TPU v7x, 128 devices: a whole 4x4x4 slice. The times are simulated.
128 devices in a mesh: dp: 8 (over z, core), label: 16 (over x, y).
Axes of the slice: x: 4, y: 4, z: 4, core: 2. Of those that a mesh axis runs over, the one named last changes fastest.
Arguments:
- texts: bfloat16 [2048, 64, 768], P(('dp', 'label')), may hold values from -6 to 6
- lengths: int32 [2048], P(('dp', 'label')), may hold values from 8 to 64, as said below
- owners: int32 [2048, 1], P(('dp', 'label')), may hold values from 0 to 15; in each aligned block of 16 rows (0 to 15, 16 to 31, ...) at most 2 rows name the same one
- gain: float32 [768], replicated, may hold values from 0.1 to 1.9
- w_in: float32 [1536, 768], replicated, may hold values from -0.21875 to 0.21875
- w_out: float32 [1536, 768], replicated, may hold values from -0.15625 to 0.15625
- free_vectors: float32 [2048, 768], P(('dp', 'label')), may hold values from -0.21875 to 0.21875
- queries: float32 [4096, 768], P('dp'), may hold values from -6 to 6
- shortlist: int32 [4096, 4], P('dp'), may hold values from 0 to 15, all different within a row
- grad_scores: float32 [4096, 4096], P('dp', 'label'), may hold values from -6 to 6
Outputs:
- scores: float32 [4096, 4096], P('dp', 'label')
- free_grad: float32 [2048, 768], P(('dp', 'label'))
- w_in_grad: float32 [1536, 768], P(('dp', 'label'))
- w_out_grad: float32 [1536, 768], P(('dp', 'label'))
Inputs may be any that keep to these rules, and one draw needn't show every extreme that they name: `lengths`: the 8 device blocks of texts that share one label index hold exactly 4608 tokens together. `owners`: among the labels of one device at most 2 share an owner, and in every draw some owner receives exactly 2 from some device. `shortlist`: each query names 4 different owners; every owner is named by some query.
All inputs are finite; a program needn't handle non-finite values.
Results may differ from a plain program's by a relative error of at most 0.0003.
Values may be sent and summed in bfloat16 or wider, within the bound.
No kernel may reach another device: no remote copies, remote signals or barrier semaphores. Data moves between devices by JAX's collectives and lax.ppermute only.
A program may use at most 128 MiB of HBM per device.

v0:
```python
import math

import jax
import jax.numpy as jnp
from jax import lax
from jax.experimental import pallas as pl
from jax.experimental.pallas import tpu as pltpu
from jax.sharding import Mesh, PartitionSpec as P

N_Z, N_CORE, N_X, N_Y = 4, 2, 4, 4
N_LABEL = N_X * N_Y
TXT = 16
LMAX = 64
D = 768
FF = 1536
HALF = FF // 2
BLOCK = FF // (N_Z * N_CORE)
ROWS = BLOCK // N_LABEL
CAP = 2
SLOTS = N_LABEL * CAP
QROWS = 512
TOKENS = 256
TEXTS_STEP = TOKENS // LMAX
STEPS = 2 * TXT // TEXTS_STEP
C0 = math.sqrt(2.0 / math.pi)
C1 = C0 * 0.044715
MIB = 1024 * 1024

f32 = jnp.float32
bf16 = jnp.bfloat16
N_CHIPS = N_Z * N_LABEL
CHIP_SLOTS = N_CHIPS * CAP
PIECES = D // 128
CHUNK = PIECES * ROWS
SLOT_ROWS = CAP * PIECES
AT_W_OUT = N_Z * CHUNK
AT_POWERS = AT_W_OUT + CHUNK
AT_LABELS = AT_POWERS + 16
SENT_ROWS = AT_LABELS + 2 * SLOT_ROWS
MOVED_ROWS = CHUNK + N_LABEL * SLOT_ROWS
LABEL_SCALE = 256.0
PARTS = 4
PART = 2 * TXT * LMAX // PARTS
LABEL = ("x", "y")


def split(value):
    high = value.astype(bf16)
    return high, (value - high.astype(f32)).astype(bf16)


def dot(a, b, dims):
    return lax.dot_general(a, b, (dims, ((), ())), preferred_element_type=f32)


def dot3(a, b, dims):
    a_high, a_low = split(a)
    b_high, b_low = split(b)
    return dot(a_high, b_high, dims) + (dot(a_high, b_low, dims) + dot(a_low, b_high, dims))


def params(mib):
    return pltpu.CompilerParams(vmem_limit_bytes=mib * MIB)


def vmem(count):
    return [pl.BlockSpec(memory_space=pltpu.VMEM)] * count


def smem(count):
    return [pl.BlockSpec(memory_space=pltpu.SMEM)] * count


def is_kept(shortlist_ref, label):
    row = jnp.max((shortlist_ref[...] == label).astype(f32), axis=0, keepdims=True)
    return jnp.broadcast_to(row, (8, QROWS)).T[:, :1]


def iota(shape, axis):
    return lax.broadcasted_iota(jnp.int32, shape, axis)


def in_hbm(value):
    return pltpu.with_memory_space_constraint(value, pltpu.HBM)


def cost(flops, nbytes):
    return pl.CostEstimate(flops=flops, bytes_accessed=nbytes, transcendentals=0)


ANY = pl.BlockSpec(memory_space=pl.ANY)
HBM = pl.BlockSpec(memory_space=pltpu.HBM)
NN, NT, TN = ((1,), (0,)), ((1,), (1,)), ((0,), (0,))


def partial_kernel(place_ref, shortlist_ref, grad_ref, queries_ref, own_ref, other_ref):
    weighted = grad_ref[...] * is_kept(shortlist_ref, place_ref[1])
    size = 2 * CHIP_SLOTS
    target = iota((size, size), 1)
    half = target // CHIP_SLOTS
    rank = target // N_CHIPS % CAP
    z = target // N_LABEL % N_Z
    lab = target % N_LABEL
    flip = jnp.where(half == 0, place_ref[0], 1 - place_ref[0])
    source = ((z * N_CORE + flip) * N_LABEL + lab) * CAP + rank
    order = (iota((size, size), 0) == source).astype(bf16)
    w_high, w_low = (dot(part, order, NN).astype(bf16) for part in split(weighted))
    q_high, q_low = split(queries_ref[...])
    total = dot(w_high, q_high, TN) + (dot(w_high, q_low, TN) + dot(w_low, q_high, TN))
    for h, ref in enumerate((own_ref, other_ref)):
        for r in range(CAP):
            start = h * CHIP_SLOTS + r * N_CHIPS
            for j in range(PIECES):
                ref[pl.ds(PIECES * r + j, N_CHIPS, stride=16)] = total[start : start + N_CHIPS, j * 128 : (j + 1) * 128]


def slot_partials(place, shortlist, grad_scores, queries):
    shape = jax.ShapeDtypeStruct((N_CHIPS * 16, 128), f32)
    return pl.pallas_call(
        partial_kernel,
        out_shape=(shape, shape),
        in_specs=smem(1) + vmem(3),
        out_specs=tuple(vmem(2)),
        compiler_params=params(24),
        cost_estimate=cost(6 * QROWS * 256 * D, 4 * 10**6),
        name="slot_partials",
    )(place, shortlist, grad_scores, queries)


def forward_kernel(
    place_ref,
    lengths_ref,
    gain_ref,
    own_ref,
    other_ref,
    w_in_ref,
    w_out_ref,
    slope_ref,
    pooled_ref,
    sums_ref,
    out_high_ref,
    out_low_ref,
    w_in_buf,
    w_out_buf,
    x_buf,
    slope_buf,
    w_high,
    w_low,
    pooled,
    pooled_x,
    w_sem,
    x_sem,
    slope_sem,
):
    core = place_ref[0]
    w_copies = [
        pltpu.make_async_copy(ref.at[:, core], buf, w_sem.at[i])
        for i, (ref, buf) in enumerate(((w_in_ref, w_in_buf), (w_out_ref, w_out_buf)))
    ]
    x_copies = [pltpu.make_async_copy(ref, x_buf.at[i], x_sem.at[i]) for i, ref in enumerate((own_ref, other_ref))]
    w_copies[0].start()
    x_copies[0].start()
    x_copies[1].start()
    w_copies[1].start()
    w_copies[0].wait()
    for z in range(N_Z):
        rows = slice(z * BLOCK, (z + 1) * BLOCK)
        w_high[rows], w_low[rows] = split(w_in_buf[z] * gain_ref[...])
    position = iota((LMAX, 1), 0)

    def store(step):
        slot = lax.rem(step, 2)
        rows = pl.ds(pl.multiple_of(step * TOKENS, TOKENS), TOKENS)
        return pltpu.make_async_copy(slope_buf.at[slot], slope_ref.at[rows], slope_sem.at[slot])

    def run(which):
        def body(s, _):
            x = x_buf[which, pl.ds(pl.multiple_of(s * TOKENS, TOKENS), TOKENS)]
            xf = x.astype(f32)
            inverse = lax.rsqrt(jnp.sum(xf * xf, axis=1, keepdims=True) * (1.0 / D) + 1e-05)
            step = which * (STEPS // 2) + s
            slot = lax.rem(step, 2)

            @pl.when(step >= 2)
            def _():
                store(step - 2).wait()

            weights = []
            for i in range(TEXTS_STEP):
                length = lengths_ref[step * TEXTS_STEP + i]
                scale = 1.0 / jnp.full((1, 1), length, jnp.int32).astype(f32)
                weights.append(jnp.where(position < length, scale, 0.0))
                rows = slice(i * LMAX, (i + 1) * LMAX)
                pooled_x[step, i : i + 1] = jnp.sum(xf[rows] * weights[i], axis=0, keepdims=True)
            weight = jnp.concatenate(weights, axis=0)
            scaled = weight * inverse
            for j in range(HALF // 256):
                cols = slice(j * 256, (j + 1) * 256)
                p = (dot(x, w_high[cols], NT) + dot(x, w_low[cols], NT)) * inverse
                p2 = p * p
                half = 0.5 + 0.5 * jnp.tanh(p * (C0 + C1 * p2))
                act = p * half
                slope = half + (act - act * half) * (2.0 * C0 + 6.0 * C1 * p2)
                slope_buf[slot, :, cols] = slope * scaled
                act = act * weight
                for i in range(TEXTS_STEP):
                    rows = slice(i * LMAX, (i + 1) * LMAX)
                    pooled[step, i : i + 1, cols] = jnp.sum(act[rows], axis=0, keepdims=True)
            store(step).start()
            return 0

        x_copies[which].wait()
        lax.fori_loop(0, STEPS // 2, body, 0)

    run(0)
    run(1)
    w_copies[1].wait()
    acts = jnp.concatenate([pooled[i] for i in range(STEPS)], axis=0)
    total = 0.5 * jnp.concatenate([pooled_x[i] for i in range(STEPS)], axis=0)
    for z in range(N_Z):
        high, low = split(w_out_buf[z])
        out_high_ref[z] = high
        out_low_ref[z] = low
        a = acts[:, z * BLOCK : (z + 1) * BLOCK]
        pooled_ref[z] = jnp.concatenate([a, jnp.zeros((2 * TXT, 256 - BLOCK), f32)], axis=1)
        a_high, a_low = split(a)
        total = total + (dot(a_high, high, NN) + (dot(a_high, low, NN) + dot(a_low, high, NN)))
    sums_ref[...] = total
    for step in (STEPS - 2, STEPS - 1):
        store(step).wait()


def forward(place, lengths, gain, own, other, w_in, w_out):
    tokens = 2 * TXT * LMAX
    shape = jax.ShapeDtypeStruct
    return pl.pallas_call(
        forward_kernel,
        out_shape=(
            pltpu.HBM((tokens, HALF), f32),
            shape((N_Z, 2 * TXT, 256), f32),
            shape((2 * TXT, D), f32),
            shape((N_Z, BLOCK, D), bf16),
            shape((N_Z, BLOCK, D), bf16),
        ),
        in_specs=smem(2) + vmem(1) + [HBM, ANY, HBM, HBM],
        out_specs=(HBM, *vmem(4)),
        scratch_shapes=[
            pltpu.VMEM((N_Z, BLOCK, D), f32),
            pltpu.VMEM((N_Z, BLOCK, D), f32),
            pltpu.VMEM((2, TXT * LMAX, D), bf16),
            pltpu.VMEM((2, TOKENS, HALF), f32),
            pltpu.VMEM((HALF, D), bf16),
            pltpu.VMEM((HALF, D), bf16),
            pltpu.VMEM((STEPS, TEXTS_STEP, HALF), f32),
            pltpu.VMEM((STEPS, TEXTS_STEP, D), f32),
            pltpu.SemaphoreType.DMA((2,)),
            pltpu.SemaphoreType.DMA((2,)),
            pltpu.SemaphoreType.DMA((2,)),
        ],
        compiler_params=params(24),
        cost_estimate=cost(10 * tokens * HALF * D, 8 * 10**6),
        name="encoder_forward",
    )(place, lengths, gain, in_hbm(own), other, in_hbm(w_in), in_hbm(w_out))


def unit_rows(sums):
    return lax.rsqrt(jnp.sum(sums * sums, axis=-1, keepdims=True) + 1e-06)


def each_label(owners_ref, counts, put):
    for o in range(N_LABEL):
        counts[o] = 0
    for i in range(TXT):
        owner = owners_ref[i]
        rank = counts[owner]
        counts[owner] = rank + 1
        put(i, owner, jnp.minimum(rank, CAP - 1))


def label_kernel(owners_ref, part_ref, came_ref, free_ref, sums_ref, out_ref, counts):
    own = part_ref[:TXT] + came_ref[TXT:]
    sums_ref[:TXT] = own
    sums_ref[TXT:] = part_ref[TXT:] + came_ref[:TXT]
    scaled = (own * unit_rows(own) + free_ref[...]) * LABEL_SCALE
    high = scaled.astype(bf16).astype(f32)
    low = scaled - high
    out_ref[...] = jnp.zeros_like(out_ref)

    def put(i, owner, rank):
        for k, value in enumerate((high, low)):
            for j in range(PIECES):
                row = pl.ds((k * CAP + rank) * PIECES + j, 1)
                out_ref[owner, row] = value[i : i + 1, j * 128 : (j + 1) * 128]

    each_label(owners_ref, counts, put)


def labels(owners, part, came, free_vectors):
    return pl.pallas_call(
        label_kernel,
        out_shape=(
            jax.ShapeDtypeStruct((2 * TXT, D), f32),
            jax.ShapeDtypeStruct((N_LABEL, 2 * SLOT_ROWS, 128), f32),
        ),
        in_specs=smem(1) + vmem(3),
        out_specs=tuple(vmem(2)),
        scratch_shapes=[pltpu.SMEM((N_LABEL,), jnp.int32)],
        compiler_params=params(8),
        cost_estimate=cost(10**6, 8 * 10**5),
        name="label_vectors",
    )(owners, part, came, free_vectors)


def scores_kernel(place_ref, shortlist_ref, queries_ref, own_ref, other_ref, out_ref):
    size = 2 * CHIP_SLOTS
    column = iota((size, size), 0)
    rank = column % CAP
    lab = column // CAP % N_LABEL
    core = column // (CAP * N_LABEL) % N_CORE
    z = column // (CAP * N_LABEL * N_CORE)
    half = jnp.where(core == place_ref[0], 0, 1)
    source = half * CHIP_SLOTS + rank * N_CHIPS + z * N_LABEL + lab
    order = (iota((size, size), 1) == source).astype(bf16)
    table = jnp.concatenate(
        [
            jnp.concatenate(
                [ref[pl.ds(PIECES * r + j, N_CHIPS, stride=SLOT_ROWS)] for j in range(PIECES)],
                axis=1,
            )
            for ref in (own_ref, other_ref)
            for r in range(CAP)
        ],
        axis=0,
    )
    t_high, t_low = (dot(order, part, NN).astype(bf16) for part in split(table))
    q_high, q_low = split(queries_ref[...])
    scores = dot(q_high, t_high, NT) + (dot(q_high, t_low, NT) + dot(q_low, t_high, NT))
    out_ref[...] = scores * is_kept(shortlist_ref, place_ref[1])


def slot_scores(place, shortlist, queries, own, other):
    return pl.pallas_call(
        scores_kernel,
        out_shape=jax.ShapeDtypeStruct((QROWS, 2 * CHIP_SLOTS), f32),
        in_specs=smem(1) + vmem(4),
        out_specs=pl.BlockSpec(memory_space=pltpu.VMEM),
        compiler_params=params(24),
        cost_estimate=cost(6 * QROWS * 256 * D, 4 * 10**6),
        name="slot_scores",
    )(place, shortlist, queries, own, other)


def return_kernel(owners_ref, came_ref, out_ref, counts):
    def put(i, owner, rank):
        value = came_ref[owner]
        for z in range(1, N_Z):
            value = value + came_ref[z * N_LABEL + owner]
        value = jnp.where(rank == 0, value[:PIECES], value[PIECES : 2 * PIECES])
        for j in range(PIECES):
            out_ref[i : i + 1, j * 128 : (j + 1) * 128] = value[j : j + 1]

    each_label(owners_ref, counts, put)


def returned(owners, came):
    return pl.pallas_call(
        return_kernel,
        out_shape=jax.ShapeDtypeStruct((TXT, D), f32),
        in_specs=smem(1) + vmem(1),
        out_specs=pl.BlockSpec(memory_space=pltpu.VMEM),
        scratch_shapes=[pltpu.SMEM((N_LABEL,), jnp.int32)],
        compiler_params=params(8),
        cost_estimate=cost(10**5, 5 * 10**5),
        name="returned_gradients",
    )(owners, came)


def pull_kernel(place_ref, free_own_ref, free_other_ref, sums_ref, high_ref, low_ref, pooled_ref, back_ref, *outs):
    free = jnp.concatenate([free_own_ref[...], free_other_ref[...]], axis=0)
    sums = sums_ref[...]
    unit = unit_rows(sums)
    along = jnp.sum(sums * free, axis=-1, keepdims=True)
    pulled = unit * free - (unit * unit * unit * along) * sums
    p_high, p_low = split(pulled)
    back_ref[...] = jnp.concatenate(
        [
            dot(p_high, high_ref[z], NT) + (dot(p_high, low_ref[z], NT) + dot(p_low, high_ref[z], NT))
            for z in range(N_Z)
        ],
        axis=1,
    )
    for f in range(N_Z):
        outs[f][:, :256] = pooled_ref[lax.rem(place_ref[4] + f, N_Z)]
        outs[f][:, 256:] = pulled


def pull(place, free_own, free_other, sums, high, low, pooled):
    return pl.pallas_call(
        pull_kernel,
        out_shape=(jax.ShapeDtypeStruct((2 * TXT, HALF), f32),)
        + (jax.ShapeDtypeStruct((2 * TXT, 256 + D), f32),) * N_Z,
        in_specs=smem(1) + vmem(6),
        out_specs=tuple(vmem(1 + N_Z)),
        compiler_params=params(12),
        cost_estimate=cost(6 * 32 * HALF * D, 3 * 10**6),
        name="pull_back",
    )(place, free_own, free_other, sums, high, low, pooled)


def backward_kernel(back_ref, gain_ref, own_ref, other_ref, slope_ref, grad, largest, x_buf, slope_buf, sem):
    copies = []
    for q in range(PARTS):
        x_rows = slice(q % (PARTS // 2) * PART, (q % (PARTS // 2) + 1) * PART)
        x_ref = (own_ref, other_ref)[q // (PARTS // 2)]
        rows = slice(q * PART, (q + 1) * PART)
        copies.append(
            (
                pltpu.make_async_copy(x_ref.at[x_rows], x_buf.at[q], sem.at[0, q]),
                pltpu.make_async_copy(slope_ref.at[rows], slope_buf.at[q], sem.at[1, q]),
            )
        )
    for pair in copies:
        for copy in pair:
            copy.start()
    for q in range(PARTS):
        for copy in copies[q]:
            copy.wait()

        def product(j, _):
            cols = pl.ds(pl.multiple_of(j * 256, 256), 256)
            total = jnp.zeros((256, D), f32)
            for i in range(PART // TOKENS):
                pieces = []
                for t in range(i * TEXTS_STEP, (i + 1) * TEXTS_STEP):
                    text = q * (PART // LMAX) + t
                    pieces.append(slope_buf[q, t * LMAX : (t + 1) * LMAX, cols] * back_ref[text : text + 1, cols])
                high, low = split(jnp.concatenate(pieces, axis=0))
                x = x_buf[q, i * TOKENS : (i + 1) * TOKENS]
                total = total + (dot(high, x, TN) + dot(low, x, TN))
            if q > 0:
                total = total + grad[cols]
            if q == PARTS - 1:
                total = total * gain_ref[...]
                largest[pl.ds(j, 1)] = jnp.max(jnp.abs(total), axis=0, keepdims=True)
            grad[cols] = total
            return 0

        lax.fori_loop(0, HALF // 256, product, 0)


def backward(back, gain, own, other, slope):
    tokens = 2 * TXT * LMAX
    shape = jax.ShapeDtypeStruct
    return pl.pallas_call(
        backward_kernel,
        out_shape=(shape((HALF, D), f32), shape((HALF // 256, D), f32)),
        in_specs=vmem(2) + [HBM, ANY, HBM],
        out_specs=tuple(vmem(2)),
        scratch_shapes=[
            pltpu.VMEM((PARTS, PART, D), bf16),
            pltpu.VMEM((PARTS, PART, HALF), f32),
            pltpu.SemaphoreType.DMA((2, PARTS)),
        ],
        compiler_params=params(24),
        cost_estimate=cost(5 * tokens * HALF * D, 4 * 10**6),
        name="encoder_backward",
    )(back, gain, in_hbm(own), other, in_hbm(slope))


def power_of(top):
    return jnp.clip(jnp.floor(14.0 - jnp.log2(jnp.maximum(top, 1e-30))), -100.0, 100.0)


def finish_kernel(grad_ref, largest_ref, labels_ref, *rest):
    factors, out_ref = rest[:N_Z], rest[N_Z]
    acts = jnp.concatenate([ref[:, :BLOCK] for ref in factors], axis=0)
    pulled = jnp.concatenate([ref[:, 256:] for ref in factors], axis=0)
    block = dot3(acts, pulled, TN)
    top = jnp.max(jnp.max(largest_ref[...], axis=0, keepdims=True), axis=1, keepdims=True)
    block_top = jnp.max(jnp.max(jnp.abs(block), axis=0, keepdims=True), axis=1, keepdims=True)
    power, block_power = power_of(top), power_of(block_top)
    scale = jnp.exp2(power)
    block = block * jnp.exp2(block_power)
    powers = jnp.concatenate([jnp.broadcast_to(power, (8, 128)), jnp.broadcast_to(block_power, (8, 128))], axis=0)
    for lab in range(N_LABEL):
        for j in range(PIECES):
            start = AT_W_OUT + j * ROWS
            out_ref[lab, start : start + ROWS] = block[lab * ROWS : (lab + 1) * ROWS, j * 128 : (j + 1) * 128]
        out_ref[lab, AT_POWERS:AT_LABELS] = powers
        out_ref[lab, AT_LABELS:] = labels_ref[lab]
    for z in range(N_Z):

        def place_rows(k, _):
            start = z * BLOCK + k * 2 * ROWS
            rows = grad_ref[pl.ds(pl.multiple_of(start, 2 * ROWS), 2 * ROWS)] * scale
            for g in range(2):
                for j in range(PIECES):
                    piece = rows[g * ROWS : (g + 1) * ROWS, j * 128 : (j + 1) * 128]
                    first = z * CHUNK + j * ROWS
                    out_ref[2 * k + g, first : first + ROWS] = piece
            return 0

        lax.fori_loop(0, N_LABEL // 2, place_rows, 0)


def finish(grad, largest, label_rows, factors):
    return pl.pallas_call(
        finish_kernel,
        out_shape=jax.ShapeDtypeStruct((N_LABEL, SENT_ROWS, 128), f32),
        in_specs=vmem(3 + N_Z),
        out_specs=pl.BlockSpec(memory_space=pltpu.VMEM),
        compiler_params=params(16),
        cost_estimate=cost(10**9, 5 * 10**6),
        name="finish_gradients",
    )(grad, largest, label_rows, *factors)


def unpieced(rows):
    return jnp.concatenate([rows[j * ROWS : (j + 1) * ROWS] for j in range(PIECES)], axis=1)


def middle_kernel(place_ref, came_ref, w_out_ref, *outs):
    total = jnp.zeros((AT_W_OUT, 128), f32)
    block = jnp.zeros((CHUNK, 128), f32)
    vectors = []
    for lab in range(N_LABEL):
        total = total + came_ref[lab, :AT_W_OUT] * jnp.exp2(-came_ref[lab, AT_POWERS : AT_POWERS + 1])
        block = block + came_ref[lab, AT_W_OUT:AT_POWERS] * jnp.exp2(-came_ref[lab, AT_POWERS + 8 : AT_POWERS + 9])
        high = came_ref[lab, AT_LABELS : AT_LABELS + SLOT_ROWS]
        low = came_ref[lab, AT_LABELS + SLOT_ROWS :]
        vectors.append((high + low) * (1.0 / LABEL_SCALE))
    w_out_ref[...] = unpieced(block)
    vectors = jnp.concatenate(vectors, axis=0)
    for f in range(N_Z):
        outs[f][CHUNK:] = vectors
    for z in range(N_Z):
        for f in range(N_Z):

            @pl.when(lax.rem(place_ref[4] + f, N_Z) == z)
            def _(z=z, f=f):
                outs[f][:CHUNK] = total[z * CHUNK : (z + 1) * CHUNK]


def middle(place, came):
    return pl.pallas_call(
        middle_kernel,
        out_shape=(jax.ShapeDtypeStruct((ROWS, D), f32),)
        + (jax.ShapeDtypeStruct((MOVED_ROWS, 128), f32),) * N_Z,
        in_specs=smem(1) + vmem(1),
        out_specs=tuple(vmem(1 + N_Z)),
        compiler_params=params(16),
        cost_estimate=cost(10**7, 4 * 10**6),
        name="plane_sums",
    )(place, came)


def last_kernel(place_ref, *rest):
    blocks, (w_in_ref, table_ref) = rest[:N_Z], rest[N_Z:]
    total = blocks[0][:CHUNK]
    for f in range(1, N_Z):
        total = total + blocks[f][:CHUNK]
    w_in_ref[...] = unpieced(total)
    size = N_LABEL * SLOT_ROWS
    for f in range(N_Z):
        z = lax.rem(place_ref[4] - f + N_Z, N_Z)
        table_ref[pl.ds(pl.multiple_of(z * size, size), size)] = blocks[f][CHUNK:]


def last(place, blocks):
    return pl.pallas_call(
        last_kernel,
        out_shape=(
            jax.ShapeDtypeStruct((ROWS, D), f32),
            jax.ShapeDtypeStruct((N_CHIPS * SLOT_ROWS, 128), f32),
        ),
        in_specs=smem(1) + vmem(N_Z),
        out_specs=tuple(vmem(2)),
        compiler_params=params(8),
        cost_estimate=cost(10**6, 10**6),
        name="z_sums",
    )(place, *blocks)


def swap(value):
    return lax.ppermute(value, "core", ((0, 1), (1, 0)))


def shift(blocks, axis):
    moved = [lax.ppermute(blocks[k], axis, [(i, (i + k) % 4) for i in range(4)]) for k in range(1, 4)]
    return [blocks[0]] + moved


def exchange(value, axes):
    return lax.all_to_all(value, axes, split_axis=0, concat_axis=0, tiled=True)


def local(texts, lengths, owners, gain, w_in, w_out, free_vectors, queries, shortlist, grad_scores):
    core, x, y, z = (lax.axis_index(name) for name in ("core", "x", "y", "z"))
    place = jnp.stack([core, x * N_Y + y, x, y, z]).astype(jnp.int32)
    own = texts.reshape(TXT * LMAX, D)
    other = swap(own)
    both_lengths = jnp.concatenate([lengths, swap(lengths)])
    owner_ids = owners[:, 0]
    names = shortlist.T
    gain_row = gain.reshape(1, D)
    w_in_blocks = w_in.reshape(N_Z, N_CORE, BLOCK, D)
    w_out_blocks = w_out.reshape(N_Z, N_CORE, BLOCK, D)

    kept, sent = slot_partials(place, names, grad_scores, queries)
    slots = exchange((kept + swap(sent)).reshape(N_CHIPS, 16, 128), ("z", "x", "y"))

    slope, pooled, part, high, low = forward(place, both_lengths, gain_row, own, other, w_in_blocks, w_out_blocks)
    sums, label_rows = labels(owner_ids, part, swap(part), free_vectors)

    free_grad = returned(owner_ids, slots)
    back, *factors = pull(place, free_grad, swap(free_grad), sums, high, low, pooled)
    factors = shift(factors, "z")
    grad, largest = backward(back, gain_row, own, other, slope)
    sent_rows = finish(grad, largest, label_rows, factors)
    came = exchange(sent_rows.astype(jnp.float16), LABEL).astype(f32)
    w_out_grad, *moved = middle(place, came)
    w_in_grad, table = last(place, shift(moved, "z"))
    scores = slot_scores(place, names, queries, table, swap(table))
    return scores, free_grad, w_in_grad, w_out_grad


def solution(mesh):
    fine = Mesh(mesh.devices.reshape(N_Z, N_CORE, N_X, N_Y), ("z", "core", "x", "y"))
    dp, every = ("z", "core"), ("z", "core", "x", "y")
    placed = (
        P(every, None, None),
        P(every),
        P(every, None),
        P(),
        P(),
        P(),
        P(every, None),
        P(dp, None),
        P(dp, None),
        P(dp, LABEL),
    )
    return jax.shard_map(
        local,
        mesh=fine,
        in_specs=placed,
        out_specs=(
            P(dp, LABEL),
            P(every, None),
            P(every, None),
            P(every, None),
        ),
        check_vma=False,
    )
```

profile of v0, /device:TPU:0, one launch (start us, length us, event | category | flops | bytes accessed | tf_op | source)
XLA Modules:
  0.0 105.3 jit_solution(487006283615172414)
XLA Ops:
  0.6 0.0 copy-start.12
  0.6 0.0 copy-start.11
  0.7 0.1 collective-permute-start.3
  0.8 0.1 stack.23.place_ref
  0.8 0.0 copy-start
  0.8 1.4 %copy-done = f32[512,768]{1,0:T(8,128)S(1)} copy-done((f32[512,768]{1,0:T(8,128)S(1)}, f32[512,768]{1,0:T(8,128)}, u32[]{:S(2)}) %copy-start) | copy-done | bytes 1572888
  2.3 0.7 copy-done.4
  2.9 0.0 copy-start.10
  2.9 1.0 copy-done.10
  4.0 2.2 %slot_partials.1 = (f32[1024,128]{1,0:T(8,128)S(1)}, f32[1024,128]{1,0:T(8,128)S(1)}) custom-call(s32[5]{0:T(128)S(1)} %stack.23.place_ref, s32[4,512]{1,0:T(4,128)S(1)} %bitcast.11, f32[512,256]{1,0:T(8,128)S(1)} %copy-done.10, f32[512,768]{1,0:T(8,128)S(1)} %copy-done), custom_call_target="tpu_custom_call" | custom-call | flops 603979776 | bytes 4000000 | tf_op jit(solution)/shard_map/slot_partials/pallas_call | solution.py:119
  6.2 0.6 collective-permute-start
  6.7 0.0 copy-done.12
  6.7 0.1 collective-permute-start.2
  6.8 0.0 copy-done.11
  6.8 1.4 %collective-permute-done.2 = s32[16]{0:T(128)S(1)} collective-permute-done((s32[16]{0:T(128)S(1)}, s32[16]{0:T(128)S(1)}, u32[]{:S(2)}, u32[]{:S(2)}) %collective-permute-start.2) | collective-permute-done | bytes 96 | tf_op jit(solution)/shard_map/ppermute | solution.py:585
  8.3 0.1 pad_add_fusion.lengths_ref
  8.4 0.0 collective-permute-done
  8.4 0.8 add.7
  9.2 11.5 %all-to-all-start = ((f32[64,16,128]{2,1,0:T(8,128)}), f32[64,16,128]{2,1,0:T(8,128)S(1)}, u32[]{:S(2)}, u32[]{:S(2)}) async-start(f32[64,16,128]{2,1,0:T(8,128)} %bitcast.7), calls=%async_computation | async-start | bytes 1048576 | tf_op jit(solution)/shard_map/all_to_all | solution.py:594
  20.7 0.0 collective-permute-done.3.other_ref
  20.7 0.0 copy-start.7
  20.7 1.1 %copy-done.7 = bf16[1024,768]{1,0:T(8,128)(2,1)} copy-done((bf16[1024,768]{1,0:T(8,128)(2,1)}, bf16[1024,768]{1,0:T(8,128)(2,1)S(1)}, u32[]{:S(2)}) %copy-start.7) | copy-done | bytes 1572888
  21.9 0.0 copy-start.8
  21.9 1.4 %copy-done.8 = bf16[1024,768]{1,0:T(8,128)(2,1)S(1)} copy-done((bf16[1024,768]{1,0:T(8,128)(2,1)S(1)}, bf16[1024,768]{1,0:T(8,128)(2,1)}, u32[]{:S(2)}) %copy-start.8) | copy-done | bytes 1572888
  23.3 0.0 copy-start.6
  23.3 14.5 %encoder_forward.1 = (f32[2048,768]{1,0:T(8,128)}, f32[4,32,256]{2,1,0:T(8,128)S(1)}, f32[32,768]{1,0:T(8,128)S(1)}, bf16[4,192,768]{2,1,0:T(8,128)(2,1)S(1)}, bf16[4,192,768]{2,1,0:T(8,128)(2,1)S(1)}) custom-call(s32[5]{0:T(128)S(1)} %stack.23.place_ref, s32[32]{0:T(128)S(1)} %pad_add_fusion.lengths_ref, f32[1,768]{1,0:T(1,128)S(1)} %reshape.24.gain_ref, ...), custom_call_target="tpu_custom_call" | custom-call | flops 12079595520 | bytes 8000000 | tf_op jit(solution)/shard_map/encoder_forward/pallas_call | solution.py:236
  37.8 0.2 collective-permute-start.4
  37.9 0.0 all-to-all-done.came_ref
  37.9 0.0 copy-done.6
  37.9 1.3 %returned_gradients.1.free_own_ref = f32[16,768]{1,0:T(8,128)} custom-call(s32[16]{0:T(128)S(1)} %bitcast.13, f32[64,16,128]{2,1,0:T(8,128)S(1)} %all-to-all-done.came_ref), custom_call_target="tpu_custom_call" | custom-call | flops 100000 | bytes 500000 | tf_op jit(solution)/shard_map/returned_gradients/pallas_call | solution.py:366
  39.2 0.4 collective-permute-start.1
  39.6 0.0 collective-permute-done.4.came_ref
  39.6 0.0 copy-done.3
  39.6 0.7 label_vectors.1
  40.3 0.4 collective-permute-done.1.free_other_ref
  40.7 0.8 copy-done.2
  41.5 1.8 %pull_back.1 = (f32[32,768]{1,0:T(8,128)S(1)}, f32[32,1024]{1,0:T(8,128)S(1)}, f32[32,1024]{1,0:T(8,128)S(1)}, f32[32,1024]{1,0:T(8,128)S(1)}, f32[32,1024]{1,0:T(8,128)S(1)}) custom-call(s32[5]{0:T(128)S(1)} %stack.23.place_ref, f32[16,768]{1,0:T(8,128)S(1)} %copy-done.2, f32[16,768]{1,0:T(8,128)S(1)} %collective-permute-done.1.free_other_ref, ...), custom_call_target="tpu_custom_call" | custom-call | flops 113246208 | bytes 3000000 | tf_op jit(solution)/shard_map/pull_back/pallas_call | solution.py:398
  43.3 1.6 %collective-permute-start.5 = (f32[32,1024]{1,0:T(8,128)S(1)}, f32[32,1024]{1,0:T(8,128)S(1)}, u32[]{:S(2)}, u32[]{:S(2)}) collective-permute-start(f32[32,1024]{1,0:T(8,128)S(1)} %get-tuple-element.40), channel_id=1, source_target_pairs={{0,32},{32,64},{64,96},{96,0},{1,33},{33,65},{65,97},{97,1},{2,34}... | collective-permute-start | bytes 393224 | tf_op jit(solution)/shard_map/ppermute | solution.py:589
  45.0 2.9 %collective-permute-start.6 = (f32[32,1024]{1,0:T(8,128)S(1)}, f32[32,1024]{1,0:T(8,128)S(1)}, u32[]{:S(2)}, u32[]{:S(2)}) collective-permute-start(f32[32,1024]{1,0:T(8,128)S(1)} %get-tuple-element.41), channel_id=1, source_target_pairs={{0,64},{32,96},{64,0},{96,32},{1,65},{33,97},{65,1},{97,33},{2,66}... | collective-permute-start | bytes 393224 | tf_op jit(solution)/shard_map/ppermute | solution.py:589
  47.8 1.4 %collective-permute-start.7 = (f32[32,1024]{1,0:T(8,128)S(1)}, f32[32,1024]{1,0:T(8,128)S(1)}, u32[]{:S(2)}, u32[]{:S(2)}) collective-permute-start(f32[32,1024]{1,0:T(8,128)S(1)} %get-tuple-element.42), channel_id=1, source_target_pairs={{0,96},{32,0},{64,32},{96,64},{1,97},{33,1},{65,33},{97,65},{2,98}... | collective-permute-start | bytes 393224 | tf_op jit(solution)/shard_map/ppermute | solution.py:589
  49.2 0.0 copy-done.9
  49.2 9.2 %encoder_backward.1 = (f32[768,768]{1,0:T(8,128)S(1)}, f32[3,768]{1,0:T(4,128)S(1)}) custom-call(f32[32,768]{1,0:T(8,128)S(1)} %get-tuple-element.34.back_ref, f32[1,768]{1,0:T(1,128)S(1)} %reshape.24.gain_ref, bf16[1024,768]{1,0:T(8,128)(2,1)} %bitcast.19, bf16[1024,768]{1,0:T(8,128)(2,1)S(1)} %copy-done.9, f32[2048,768]{1,0:T(8,128)} %get-tuple-element.35.slope_ref), custom_call_target="tpu_custom_call" | custom-call | flops 6039797760 | bytes 4000000 | tf_op jit(solution)/shard_map/encoder_backward/pallas_call | solution.py:454
  58.4 0.0 collective-permute-done.5.rest_1_
  58.4 0.0 collective-permute-done.6.rest_2_
  58.4 0.0 collective-permute-done.7.rest_3_
  58.5 0.9 finish_gradients.1
  59.4 0.2 convert_element_type.6
  59.6 29.8 %all_to_all.10 = f16[16,400,128]{2,1,0:T(8,128)(2,1)S(1)} all-to-all(f16[16,400,128]{2,1,0:T(8,128)(2,1)S(1)} %convert_element_type.6), channel_id=1, replica_groups=mesh['z'=4,'core'=2,'x'=4,'y'=4] {'x','y'}, dimensions={0} | all-to-all | bytes 3276800 | tf_op jit(solution)/shard_map/all_to_all | solution.py:594
  89.3 0.2 convert_element_type.7.came_ref
  89.6 0.0 copy-start.1
  89.6 0.0 copy-start.5
  89.6 1.7 %plane_sums.1 = (f32[12,768]{1,0:T(8,128)}, f32[264,128]{1,0:T(8,128)S(1)}, f32[264,128]{1,0:T(8,128)S(1)}, f32[264,128]{1,0:T(8,128)S(1)}, f32[264,128]{1,0:T(8,128)S(1)}) custom-call(s32[5]{0:T(128)S(1)} %stack.23.place_ref, f32[16,400,128]{2,1,0:T(8,128)S(1)} %convert_element_type.7.came_ref), custom_call_target="tpu_custom_call" | custom-call | flops 10000000 | bytes 4000000 | tf_op jit(solution)/shard_map/plane_sums/pallas_call | solution.py:545
  91.2 0.6 collective-permute-start.8
  91.9 1.3 %collective-permute-start.9 = (f32[264,128]{1,0:T(8,128)S(1)}, f32[264,128]{1,0:T(8,128)S(1)}, u32[]{:S(2)}, u32[]{:S(2)}) collective-permute-start(f32[264,128]{1,0:T(8,128)S(1)} %get-tuple-element.45), channel_id=1, source_target_pairs={{0,64},{32,96},{64,0},{96,32},{1,65},{33,97},{65,1},{97,33},{2,66}... | collective-permute-start | bytes 405512 | tf_op jit(solution)/shard_map/ppermute | solution.py:589
  93.2 1.4 %collective-permute-start.10 = (f32[264,128]{1,0:T(8,128)S(1)}, f32[264,128]{1,0:T(8,128)S(1)}, u32[]{:S(2)}, u32[]{:S(2)}) collective-permute-start(f32[264,128]{1,0:T(8,128)S(1)} %get-tuple-element.46), channel_id=1, source_target_pairs={{0,96},{32,0},{64,32},{96,64},{1,97},{33,1},{65,33},{97,65},{2,98}... | collective-permute-start | bytes 405512 | tf_op jit(solution)/shard_map/ppermute | solution.py:589
  94.6 4.3 %collective-permute-done.8.rest_1_ = f32[264,128]{1,0:T(8,128)S(1)} collective-permute-done((f32[264,128]{1,0:T(8,128)S(1)}, f32[264,128]{1,0:T(8,128)S(1)}, u32[]{:S(2)}, u32[]{:S(2)}) %collective-permute-start.8) | collective-permute-done | bytes 135200 | tf_op jit(solution)/shard_map/ppermute | solution.py:589
  98.9 0.0 collective-permute-done.9.rest_2_
  98.9 0.9 collective-permute-done.10.rest_3_
  99.8 1.2 %z_sums.1 = (f32[12,768]{1,0:T(8,128)}, f32[768,128]{1,0:T(8,128)S(1)}) custom-call(s32[5]{0:T(128)S(1)} %stack.23.place_ref, f32[264,128]{1,0:T(8,128)S(1)} %get-tuple-element.43.rest_0_, f32[264,128]{1,0:T(8,128)S(1)} %collective-permute-done.8.rest_1_, f32[264,128]{1,0:T(8,128)S(1)} %collective-permute-done.9.rest_2_, ...), custom_call_target="tpu_custom_call" | custom-call | flops 1000000 | bytes 1000000 | tf_op jit(solution)/shard_map/z_sums/pallas_call | solution.py:570
  101.0 0.0 collective-permute-start.11
  101.0 1.7 %collective-permute-done.11.other_ref = f32[768,128]{1,0:T(8,128)S(1)} collective-permute-done((f32[768,128]{1,0:T(8,128)S(1)}, f32[768,128]{1,0:T(8,128)S(1)}, u32[]{:S(2)}, u32[]{:S(2)}) %collective-permute-start.11) | collective-permute-done | bytes 393248 | tf_op jit(solution)/shard_map/ppermute | solution.py:585
  102.7 0.0 copy-done.1
  102.7 0.0 copy-done.5
  102.8 2.5 %slot_scores.1 = f32[512,256]{1,0:T(8,128)} custom-call(s32[5]{0:T(128)S(1)} %stack.23.place_ref, s32[4,512]{1,0:T(4,128)S(1)} %bitcast.12, f32[512,768]{1,0:T(8,128)S(1)} %copy-done.1, f32[768,128]{1,0:T(8,128)S(1)} %get-tuple-element.47.own_ref, f32[768,128]{1,0:T(8,128)S(1)} %collective-permute-done.11.other_ref), custom_call_target="tpu_custom_call" | custom-call | flops 603979776 | bytes 4000000 | tf_op jit(solution)/shard_map/slot_scores/pallas_call | solution.py:342
  (5 shorter events, 0.0 us)
Async XLA Ops:
  0.6 6.1 %copy-start.12 = (s32[16]{0:T(128)S(1)}, s32[16]{0:T(128)}, u32[]{:S(2)}) copy-start(s32[16]{0:T(128)} %param.11) | copy-start | bytes 196
  0.6 6.2 %copy-start.11 = (f32[768]{0:T(1024)S(1)}, f32[768]{0:T(1024)}, u32[]{:S(2)}) copy-start(f32[768]{0:T(1024)} %param.13) | copy-start | bytes 9220
  0.7 20.1 %collective-permute-start.3 = (bf16[1024,768]{1,0:T(8,128)(2,1)}, bf16[1024,768]{1,0:T(8,128)(2,1)S(1)}, u32[]{:S(2)}, u32[]{:S(2)}) collective-permute-start(bf16[1024,768]{1,0:T(8,128)(2,1)} %bitcast.17), channel_id=1, source_target_pairs={{0,16},{16,0},{1,17},{17,1},{2,18},{18,2},{3,19},{19,3},{4,20},{20... | collective-permute-start | bytes 4718600 | tf_op jit(solution)/shard_map/ppermute | solution.py:585
  0.8 1.4 %copy-start = (f32[512,768]{1,0:T(8,128)S(1)}, f32[512,768]{1,0:T(8,128)}, u32[]{:S(2)}) copy-start(f32[512,768]{1,0:T(8,128)} %queries_ref.3) | copy-start | bytes 4718596
  2.2 0.7 copy-start.4
  2.9 1.0 copy-start.10
  6.2 2.2 %collective-permute-start = (f32[1024,128]{1,0:T(8,128)S(1)}, f32[1024,128]{1,0:T(8,128)S(1)}, u32[]{:S(2)}, u32[]{:S(2)}) collective-permute-start(f32[1024,128]{1,0:T(8,128)S(1)} %get-tuple-element.28), channel_id=1, source_target_pairs={{0,16},{16,0},{1,17},{17,1},{2,18},{18,2},{3,19},{19,3},{4,20},{20... | collective-permute-start | bytes 1572872 | tf_op jit(solution)/shard_map/ppermute | solution.py:585
  6.7 1.5 %collective-permute-start.2 = (s32[16]{0:T(128)S(1)}, s32[16]{0:T(128)S(1)}, u32[]{:S(2)}, u32[]{:S(2)}) collective-permute-start(s32[16]{0:T(128)S(1)} %copy-done.12), channel_id=1, source_target_pairs={{0,16},{16,0},{1,17},{17,1},{2,18},{18,2},{3,19},{19,3},{4,20},{20... | collective-permute-start | bytes 200 | tf_op jit(solution)/shard_map/ppermute | solution.py:585
  9.2 28.7 %all-to-all-start = ((f32[64,16,128]{2,1,0:T(8,128)}), f32[64,16,128]{2,1,0:T(8,128)S(1)}, u32[]{:S(2)}, u32[]{:S(2)}) async-start(f32[64,16,128]{2,1,0:T(8,128)} %bitcast.7), calls=%async_computation | async-start | bytes 1048576 | tf_op jit(solution)/shard_map/all_to_all | solution.py:594
  20.7 1.1 %copy-start.7 = (bf16[1024,768]{1,0:T(8,128)(2,1)}, bf16[1024,768]{1,0:T(8,128)(2,1)S(1)}, u32[]{:S(2)}) copy-start(bf16[1024,768]{1,0:T(8,128)(2,1)S(1)} %collective-permute-done.3.other_ref) | copy-start | bytes 4718596
  21.9 1.4 %copy-start.8 = (bf16[1024,768]{1,0:T(8,128)(2,1)S(1)}, bf16[1024,768]{1,0:T(8,128)(2,1)}, u32[]{:S(2)}) copy-start(bf16[1024,768]{1,0:T(8,128)(2,1)} %copy-done.7) | copy-start | bytes 4718596
  23.3 14.6 %copy-start.6 = (s32[16,1]{0,1:T(1,128)S(1)}, s32[16,1]{0,1:T(1,128)}, u32[]{:S(2)}) copy-start(s32[16,1]{0,1:T(1,128)} %param.12) | copy-start | bytes 196
  23.3 16.3 %copy-start.3 = (f32[16,768]{1,0:T(8,128)S(1)}, f32[16,768]{1,0:T(8,128)}, u32[]{:S(2)}) copy-start(f32[16,768]{1,0:T(8,128)} %free_ref.1) | copy-start | bytes 147460
  37.8 1.9 %collective-permute-start.4 = (f32[32,768]{1,0:T(8,128)S(1)}, f32[32,768]{1,0:T(8,128)S(1)}, u32[]{:S(2)}, u32[]{:S(2)}) collective-permute-start(f32[32,768]{1,0:T(8,128)S(1)} %get-tuple-element.29.part_ref), channel_id=1, source_target_pairs={{0,16},{16,0},{1,17},{17,1},{2,18},{18,2},{3,19},{19,3},{4,20},{20... | collective-permute-start | bytes 294920 | tf_op jit(solution)/shard_map/ppermute | solution.py:585
  39.2 1.5 %collective-permute-start.1 = (f32[16,768]{1,0:T(8,128)}, f32[16,768]{1,0:T(8,128)S(1)}, u32[]{:S(2)}, u32[]{:S(2)}) collective-permute-start(f32[16,768]{1,0:T(8,128)} %returned_gradients.1.free_own_ref), channel_id=1, source_target_pairs={{0,16},{16,0},{1,17},{17,1},{2,18},{18,2},{3,19},{19,3},{4,20},{20... | collective-permute-start | bytes 147464 | tf_op jit(solution)/shard_map/ppermute | solution.py:585
  40.7 0.8 copy-start.2
  41.5 7.7 %copy-start.9 = (bf16[1024,768]{1,0:T(8,128)(2,1)S(1)}, bf16[1024,768]{1,0:T(8,128)(2,1)}, u32[]{:S(2)}) copy-start(bf16[1024,768]{1,0:T(8,128)(2,1)} %copy-done.7) | copy-start | bytes 4718596
  43.3 15.1 %collective-permute-start.5 = (f32[32,1024]{1,0:T(8,128)S(1)}, f32[32,1024]{1,0:T(8,128)S(1)}, u32[]{:S(2)}, u32[]{:S(2)}) collective-permute-start(f32[32,1024]{1,0:T(8,128)S(1)} %get-tuple-element.40), channel_id=1, source_target_pairs={{0,32},{32,64},{64,96},{96,0},{1,33},{33,65},{65,97},{97,1},{2,34}... | collective-permute-start | bytes 393224 | tf_op jit(solution)/shard_map/ppermute | solution.py:589
  45.0 13.5 %collective-permute-start.6 = (f32[32,1024]{1,0:T(8,128)S(1)}, f32[32,1024]{1,0:T(8,128)S(1)}, u32[]{:S(2)}, u32[]{:S(2)}) collective-permute-start(f32[32,1024]{1,0:T(8,128)S(1)} %get-tuple-element.41), channel_id=1, source_target_pairs={{0,64},{32,96},{64,0},{96,32},{1,65},{33,97},{65,1},{97,33},{2,66}... | collective-permute-start | bytes 393224 | tf_op jit(solution)/shard_map/ppermute | solution.py:589
  47.8 10.6 %collective-permute-start.7 = (f32[32,1024]{1,0:T(8,128)S(1)}, f32[32,1024]{1,0:T(8,128)S(1)}, u32[]{:S(2)}, u32[]{:S(2)}) collective-permute-start(f32[32,1024]{1,0:T(8,128)S(1)} %get-tuple-element.42), channel_id=1, source_target_pairs={{0,96},{32,0},{64,32},{96,64},{1,97},{33,1},{65,33},{97,65},{2,98}... | collective-permute-start | bytes 393224 | tf_op jit(solution)/shard_map/ppermute | solution.py:589
  89.6 13.2 %copy-start.1 = (f32[512,768]{1,0:T(8,128)S(1)}, f32[512,768]{1,0:T(8,128)}, u32[]{:S(2)}) copy-start(f32[512,768]{1,0:T(8,128)} %queries_ref.3) | copy-start | bytes 4718596
  89.6 13.2 %copy-start.5 = (s32[512,4]{0,1:T(4,128)S(1)}, s32[512,4]{0,1:T(4,128)}, u32[]{:S(2)}) copy-start(s32[512,4]{0,1:T(4,128)} %param.18) | copy-start | bytes 24580
  91.2 7.7 %collective-permute-start.8 = (f32[264,128]{1,0:T(8,128)S(1)}, f32[264,128]{1,0:T(8,128)S(1)}, u32[]{:S(2)}, u32[]{:S(2)}) collective-permute-start(f32[264,128]{1,0:T(8,128)S(1)} %get-tuple-element.44), channel_id=1, source_target_pairs={{0,32},{32,64},{64,96},{96,0},{1,33},{33,65},{65,97},{97,1},{2,34}... | collective-permute-start | bytes 405512 | tf_op jit(solution)/shard_map/ppermute | solution.py:589
  91.9 7.0 %collective-permute-start.9 = (f32[264,128]{1,0:T(8,128)S(1)}, f32[264,128]{1,0:T(8,128)S(1)}, u32[]{:S(2)}, u32[]{:S(2)}) collective-permute-start(f32[264,128]{1,0:T(8,128)S(1)} %get-tuple-element.45), channel_id=1, source_target_pairs={{0,64},{32,96},{64,0},{96,32},{1,65},{33,97},{65,1},{97,33},{2,66}... | collective-permute-start | bytes 405512 | tf_op jit(solution)/shard_map/ppermute | solution.py:589
  93.2 6.6 %collective-permute-start.10 = (f32[264,128]{1,0:T(8,128)S(1)}, f32[264,128]{1,0:T(8,128)S(1)}, u32[]{:S(2)}, u32[]{:S(2)}) collective-permute-start(f32[264,128]{1,0:T(8,128)S(1)} %get-tuple-element.46), channel_id=1, source_target_pairs={{0,96},{32,0},{64,32},{96,64},{1,97},{33,1},{65,33},{97,65},{2,98}... | collective-permute-start | bytes 405512 | tf_op jit(solution)/shard_map/ppermute | solution.py:589
  101.0 1.7 %collective-permute-start.11 = (f32[768,128]{1,0:T(8,128)S(1)}, f32[768,128]{1,0:T(8,128)S(1)}, u32[]{:S(2)}, u32[]{:S(2)}) collective-permute-start(f32[768,128]{1,0:T(8,128)S(1)} %get-tuple-element.47.own_ref), channel_id=1, source_target_pairs={{0,16},{16,0},{1,17},{17,1},{2,18},{18,2},{3,19},{19,3},{4,20},{20... | collective-permute-start | bytes 1179656 | tf_op jit(solution)/shard_map/ppermute | solution.py:585
where the time goes:
time: 107 us; the launch traced here: 105 us
  Pallas kernels  35.9 us (34%)
  blocking collectives  29.8 us (28%)
  starting transfers between devices  22 us (21%)
  waiting for transfers between devices  8.8 us (8%)
  local copies, waits for them, and re-layouts  6.61 us (6%)
  other arithmetic  1.35 us (1%)
    all_to_all x1, blocking collectives, exchange(): return lax.all_to_all(value, axes, split_axis=0, concat_axis=0, tiled=True)  29.8 us
    pallas_call x1, Pallas kernels, forward(): pl.pallas_call(forward_kernel, out_shape=(pltpu.HBM((tokens, HALF), f32),...  14.5 us
    all_to_all x1, starting transfers between devices, exchange(): return lax.all_to_all(value, axes, split_axis=0, concat_axis=0, tiled=True)  11.5 us
    pallas_call x1, Pallas kernels, backward(): pl.pallas_call(backward_kernel, out_shape=(shape((HALF, D), f32), shape((...  9.24 us
    ppermute x6, starting transfers between devices, shift(): lax.ppermute(blocks[k], axis, [(i, (i + k) % 4) for i in range(4)])  9.17 us
    unnamed x26, local copies, waits for them, and re-layouts  6.52 us
    ppermute x6, waiting for transfers between devices, shift(): lax.ppermute(blocks[k], axis, [(i, (i + k) % 4) for i in range(4)])  5.26 us
    ppermute x6, waiting for transfers between devices, swap(): return lax.ppermute(value, 'core', ((0, 1), (1, 0)))  3.55 us
  transfers between devices with their start and end apart: 13, of which 5 were waited for; matrix products, arithmetic and copies ran while one was open for 1% of the time, Pallas kernels for 26%

commit v1 on v0

--- a/solution.py
+++ b/solution.py
@@ -1,3 +1,4 @@
+import functools
 import math
 
 import jax
@@ -35,11 +36,12 @@
 SLOT_ROWS = CAP * PIECES
 AT_W_OUT = N_Z * CHUNK
 AT_POWERS = AT_W_OUT + CHUNK
-AT_LABELS = AT_POWERS + 16
-SENT_ROWS = AT_LABELS + 2 * SLOT_ROWS
-MOVED_ROWS = CHUNK + N_LABEL * SLOT_ROWS
+AT_LABELS = AT_POWERS + 8
+SENT_ROWS = AT_LABELS + N_Z * SLOT_ROWS
+FACTOR_ROWS = 2 * TXT * (256 + D) // 128
+MOVED_ROWS = FACTOR_ROWS + N_LABEL * SLOT_ROWS
 LABEL_SCALE = 256.0
-PARTS = 4
+PARTS = 2
 PART = 2 * TXT * LMAX // PARTS
 LABEL = ("x", "y")
 
@@ -124,7 +126,7 @@
         compiler_params=params(24),
         cost_estimate=cost(6 * QROWS * 256 * D, 4 * 10**6),
         name="slot_partials",
-    )(place, shortlist, grad_scores, queries)
+    )(place, in_hbm(shortlist), in_hbm(grad_scores), in_hbm(queries))
 
 
 def forward_kernel(
@@ -143,7 +145,10 @@
     w_in_buf,
     w_out_buf,
     x_buf,
-    slope_buf,
+    slope_even,
+    slope_odd,
+    keep_even,
+    keep_odd,
     w_high,
     w_low,
     pooled,
@@ -160,60 +165,68 @@
     x_copies = [pltpu.make_async_copy(ref, x_buf.at[i], x_sem.at[i]) for i, ref in enumerate((own_ref, other_ref))]
     w_copies[0].start()
     x_copies[0].start()
+    w_copies[0].wait()
     x_copies[1].start()
     w_copies[1].start()
-    w_copies[0].wait()
     for z in range(N_Z):
         rows = slice(z * BLOCK, (z + 1) * BLOCK)
         w_high[rows], w_low[rows] = split(w_in_buf[z] * gain_ref[...])
     position = iota((LMAX, 1), 0)
 
-    def store(step):
-        slot = lax.rem(step, 2)
-        rows = pl.ds(pl.multiple_of(step * TOKENS, TOKENS), TOKENS)
-        return pltpu.make_async_copy(slope_buf.at[slot], slope_ref.at[rows], slope_sem.at[slot])
-
-    def run(which):
-        def body(s, _):
-            x = x_buf[which, pl.ds(pl.multiple_of(s * TOKENS, TOKENS), TOKENS)]
-            xf = x.astype(f32)
-            inverse = lax.rsqrt(jnp.sum(xf * xf, axis=1, keepdims=True) * (1.0 / D) + 1e-05)
-            step = which * (STEPS // 2) + s
-            slot = lax.rem(step, 2)
-
-            @pl.when(step >= 2)
-            def _():
-                store(step - 2).wait()
-
-            weights = []
+    keeps, slope_bufs = (keep_even, keep_odd), (slope_even, slope_odd)
+
+    def store_from(buf, parity, step):
+        rows = slice(step * TOKENS, (step + 1) * TOKENS)
+        return pltpu.make_async_copy(buf, slope_ref.at[rows], slope_sem.at[parity])
+
+    def tokens_of(step):
+        start = step % (STEPS // 2) * TOKENS
+        return x_buf[step // (STEPS // 2), start : start + TOKENS]
+
+    def product(step, keep):
+        x = tokens_of(step)
+        for j in range(HALF // 256):
+            cols = slice(j * 256, (j + 1) * 256)
+            keep[:, cols] = dot(x, w_high[cols], NT) + dot(x, w_low[cols], NT)
+
+    def turn(step, now, later, slope_out, copy):
+        if step >= 2:
+            copy(step - 2).wait()
+        if step + 1 < STEPS:
+            product(step + 1, later)
+        xf = tokens_of(step).astype(f32)
+        inverse = lax.rsqrt(jnp.sum(xf * xf, axis=1, keepdims=True) * (1.0 / D) + 1e-05)
+        weights = []
+        for i in range(TEXTS_STEP):
+            length = lengths_ref[step * TEXTS_STEP + i]
+            scale = 1.0 / jnp.full((1, 1), length, jnp.int32).astype(f32)
+            weights.append(jnp.where(position < length, scale, 0.0))
+            rows = slice(i * LMAX, (i + 1) * LMAX)
+            pooled_x[step, i : i + 1] = jnp.sum(xf[rows] * weights[i], axis=0, keepdims=True)
+        weight = jnp.concatenate(weights, axis=0)
+        scaled = weight * inverse
+        for j in range(HALF // 256):
+            cols = slice(j * 256, (j + 1) * 256)
+            p = now[:, cols] * inverse
+            p2 = p * p
+            half = 0.5 + 0.5 * jnp.tanh(p * (C0 + C1 * p2))
+            act = p * half
+            slope = half + (act - act * half) * (2.0 * C0 + 6.0 * C1 * p2)
+            slope_out[:, cols] = slope * scaled
+            act = act * weight
             for i in range(TEXTS_STEP):
-                length = lengths_ref[step * TEXTS_STEP + i]
-                scale = 1.0 / jnp.full((1, 1), length, jnp.int32).astype(f32)
-                weights.append(jnp.where(position < length, scale, 0.0))
                 rows = slice(i * LMAX, (i + 1) * LMAX)
-                pooled_x[step, i : i + 1] = jnp.sum(xf[rows] * weights[i], axis=0, keepdims=True)
-            weight = jnp.concatenate(weights, axis=0)
-            scaled = weight * inverse
-            for j in range(HALF // 256):
-                cols = slice(j * 256, (j + 1) * 256)
-                p = (dot(x, w_high[cols], NT) + dot(x, w_low[cols], NT)) * inverse
-                p2 = p * p
-                half = 0.5 + 0.5 * jnp.tanh(p * (C0 + C1 * p2))
-                act = p * half
-                slope = half + (act - act * half) * (2.0 * C0 + 6.0 * C1 * p2)
-                slope_buf[slot, :, cols] = slope * scaled
-                act = act * weight
-                for i in range(TEXTS_STEP):
-                    rows = slice(i * LMAX, (i + 1) * LMAX)
-                    pooled[step, i : i + 1, cols] = jnp.sum(act[rows], axis=0, keepdims=True)
-            store(step).start()
-            return 0
-
-        x_copies[which].wait()
-        lax.fori_loop(0, STEPS // 2, body, 0)
-
-    run(0)
-    run(1)
+                pooled[step, i : i + 1, cols] = jnp.sum(act[rows], axis=0, keepdims=True)
+        copy(step).start()
+
+    x_copies[0].wait()
+    product(0, keeps[0])
+    for step in range(STEPS):
+        if step == STEPS // 2 - 1:
+            x_copies[1].wait()
+        parity = step % 2
+        store = functools.partial(store_from, slope_bufs[parity], parity)
+        turn(step, keeps[parity], keeps[1 - parity], slope_bufs[parity], store)
     w_copies[1].wait()
     acts = jnp.concatenate([pooled[i] for i in range(STEPS)], axis=0)
     total = 0.5 * jnp.concatenate([pooled_x[i] for i in range(STEPS)], axis=0)
@@ -226,8 +239,8 @@
         a_high, a_low = split(a)
         total = total + (dot(a_high, high, NN) + (dot(a_high, low, NN) + dot(a_low, high, NN)))
     sums_ref[...] = total
-    for step in (STEPS - 2, STEPS - 1):
-        store(step).wait()
+    for parity in range(2):
+        store_from(slope_bufs[parity], parity, STEPS - 2 + parity).wait()
 
 
 def forward(place, lengths, gain, own, other, w_in, w_out):
@@ -242,13 +255,16 @@
             shape((N_Z, BLOCK, D), bf16),
             shape((N_Z, BLOCK, D), bf16),
         ),
-        in_specs=smem(2) + vmem(1) + [HBM, ANY, HBM, HBM],
+        in_specs=smem(2) + vmem(1) + [HBM] * 4,
         out_specs=(HBM, *vmem(4)),
         scratch_shapes=[
             pltpu.VMEM((N_Z, BLOCK, D), f32),
             pltpu.VMEM((N_Z, BLOCK, D), f32),
             pltpu.VMEM((2, TXT * LMAX, D), bf16),
-            pltpu.VMEM((2, TOKENS, HALF), f32),
+            pltpu.VMEM((TOKENS, HALF), f32),
+            pltpu.VMEM((TOKENS, HALF), f32),
+            pltpu.VMEM((TOKENS, HALF), f32),
+            pltpu.VMEM((TOKENS, HALF), f32),
             pltpu.VMEM((HALF, D), bf16),
             pltpu.VMEM((HALF, D), bf16),
             pltpu.VMEM((STEPS, TEXTS_STEP, HALF), f32),
@@ -260,7 +276,7 @@
         compiler_params=params(24),
         cost_estimate=cost(10 * tokens * HALF * D, 8 * 10**6),
         name="encoder_forward",
-    )(place, lengths, gain, in_hbm(own), other, in_hbm(w_in), in_hbm(w_out))
+    )(place, lengths, gain, in_hbm(own), in_hbm(other), in_hbm(w_in), in_hbm(w_out))
 
 
 def unit_rows(sums):
@@ -282,15 +298,12 @@
     sums_ref[:TXT] = own
     sums_ref[TXT:] = part_ref[TXT:] + came_ref[:TXT]
     scaled = (own * unit_rows(own) + free_ref[...]) * LABEL_SCALE
-    high = scaled.astype(bf16).astype(f32)
-    low = scaled - high
     out_ref[...] = jnp.zeros_like(out_ref)
 
     def put(i, owner, rank):
-        for k, value in enumerate((high, low)):
-            for j in range(PIECES):
-                row = pl.ds((k * CAP + rank) * PIECES + j, 1)
-                out_ref[owner, row] = value[i : i + 1, j * 128 : (j + 1) * 128]
+        first = owner // 8 * (8 * SLOT_ROWS) + rank * (8 * PIECES) + lax.rem(owner, 8)
+        for j in range(PIECES):
+            out_ref[pl.ds(first + 8 * j, 1)] = scaled[i : i + 1, j * 128 : (j + 1) * 128]
 
     each_label(owners_ref, counts, put)
 
@@ -300,7 +313,7 @@
         label_kernel,
         out_shape=(
             jax.ShapeDtypeStruct((2 * TXT, D), f32),
-            jax.ShapeDtypeStruct((N_LABEL, 2 * SLOT_ROWS, 128), f32),
+            jax.ShapeDtypeStruct((N_LABEL * SLOT_ROWS, 128), f32),
         ),
         in_specs=smem(1) + vmem(3),
         out_specs=tuple(vmem(2)),
@@ -350,7 +363,7 @@
     )(place, shortlist, queries, own, other)
 
 
-def return_kernel(owners_ref, came_ref, out_ref, counts):
+def return_kernel(owners_ref, came_ref, out_ref, again_ref, counts):
     def put(i, owner, rank):
         value = came_ref[owner]
         for z in range(1, N_Z):
@@ -358,6 +371,7 @@
         value = jnp.where(rank == 0, value[:PIECES], value[PIECES : 2 * PIECES])
         for j in range(PIECES):
             out_ref[i : i + 1, j * 128 : (j + 1) * 128] = value[j : j + 1]
+            again_ref[i : i + 1, j * 128 : (j + 1) * 128] = value[j : j + 1]
 
     each_label(owners_ref, counts, put)
 
@@ -365,9 +379,9 @@
 def returned(owners, came):
     return pl.pallas_call(
         return_kernel,
-        out_shape=jax.ShapeDtypeStruct((TXT, D), f32),
+        out_shape=(jax.ShapeDtypeStruct((TXT, D), f32),) * 2,
         in_specs=smem(1) + vmem(1),
-        out_specs=pl.BlockSpec(memory_space=pltpu.VMEM),
+        out_specs=tuple(vmem(2)),
         scratch_shapes=[pltpu.SMEM((N_LABEL,), jnp.int32)],
         compiler_params=params(8),
         cost_estimate=cost(10**5, 5 * 10**5),
@@ -375,7 +389,7 @@
     )(owners, came)
 
 
-def pull_kernel(place_ref, free_own_ref, free_other_ref, sums_ref, high_ref, low_ref, pooled_ref, back_ref, *outs):
+def pull_kernel(place_ref, free_own_ref, free_other_ref, sums_ref, high_ref, low_ref, pooled_ref, labels_ref, back_ref, *outs):
     free = jnp.concatenate([free_own_ref[...], free_other_ref[...]], axis=0)
     sums = sums_ref[...]
     unit = unit_rows(sums)
@@ -390,21 +404,24 @@
         axis=1,
     )
     for f in range(N_Z):
-        outs[f][:, :256] = pooled_ref[lax.rem(place_ref[4] + f, N_Z)]
-        outs[f][:, 256:] = pulled
-
-
-def pull(place, free_own, free_other, sums, high, low, pooled):
+        acts = pooled_ref[lax.rem(place_ref[4] + f, N_Z)]
+        for k in range(FACTOR_ROWS // (2 * TXT)):
+            piece = acts[:, k * 128 : (k + 1) * 128] if k < 2 else pulled[:, (k - 2) * 128 : (k - 1) * 128]
+            outs[f][k * 2 * TXT : (k + 1) * 2 * TXT] = piece
+        outs[f][FACTOR_ROWS:] = labels_ref[...]
+
+
+def pull(place, free_own, free_other, sums, high, low, pooled, label_rows):
     return pl.pallas_call(
         pull_kernel,
         out_shape=(jax.ShapeDtypeStruct((2 * TXT, HALF), f32),)
-        + (jax.ShapeDtypeStruct((2 * TXT, 256 + D), f32),) * N_Z,
-        in_specs=smem(1) + vmem(6),
+        + (jax.ShapeDtypeStruct((MOVED_ROWS, 128), f32),) * N_Z,
+        in_specs=smem(1) + vmem(7),
         out_specs=tuple(vmem(1 + N_Z)),
         compiler_params=params(12),
         cost_estimate=cost(6 * 32 * HALF * D, 3 * 10**6),
         name="pull_back",
-    )(place, free_own, free_other, sums, high, low, pooled)
+    )(place, free_own, free_other, sums, high, low, pooled, label_rows)
 
 
 def backward_kernel(back_ref, gain_ref, own_ref, other_ref, slope_ref, grad, largest, x_buf, slope_buf, sem):
@@ -419,15 +436,17 @@
                 pltpu.make_async_copy(slope_ref.at[rows], slope_buf.at[q], sem.at[1, q]),
             )
         )
-    for pair in copies:
-        for copy in pair:
-            copy.start()
+    for copy in copies[0]:
+        copy.start()
     for q in range(PARTS):
         for copy in copies[q]:
             copy.wait()
-
-        def product(j, _):
-            cols = pl.ds(pl.multiple_of(j * 256, 256), 256)
+        if q + 1 < PARTS:
+            for copy in copies[q + 1]:
+                copy.start()
+
+        def product(j):
+            cols = slice(j * 256, (j + 1) * 256)
             total = jnp.zeros((256, D), f32)
             for i in range(PART // TOKENS):
                 pieces = []
@@ -441,11 +460,11 @@
                 total = total + grad[cols]
             if q == PARTS - 1:
                 total = total * gain_ref[...]
-                largest[pl.ds(j, 1)] = jnp.max(jnp.abs(total), axis=0, keepdims=True)
+                largest[j : j + 1] = jnp.max(jnp.abs(total), axis=0, keepdims=True)
             grad[cols] = total
-            return 0
-
-        lax.fori_loop(0, HALF // 256, product, 0)
+
+        for j in range(HALF // 256):
+            product(j)
 
 
 def backward(back, gain, own, other, slope):
@@ -454,7 +473,7 @@
     return pl.pallas_call(
         backward_kernel,
         out_shape=(shape((HALF, D), f32), shape((HALF // 256, D), f32)),
-        in_specs=vmem(2) + [HBM, ANY, HBM],
+        in_specs=vmem(2) + [HBM] * 3,
         out_specs=tuple(vmem(2)),
         scratch_shapes=[
             pltpu.VMEM((PARTS, PART, D), bf16),
@@ -464,121 +483,121 @@
         compiler_params=params(24),
         cost_estimate=cost(5 * tokens * HALF * D, 4 * 10**6),
         name="encoder_backward",
-    )(back, gain, in_hbm(own), other, in_hbm(slope))
+    )(back, gain, in_hbm(own), in_hbm(other), in_hbm(slope))
 
 
 def power_of(top):
     return jnp.clip(jnp.floor(14.0 - jnp.log2(jnp.maximum(top, 1e-30))), -100.0, 100.0)
 
 
-def finish_kernel(grad_ref, largest_ref, labels_ref, *rest):
+def finish_kernel(grad_ref, largest_ref, *rest):
     factors, out_ref = rest[:N_Z], rest[N_Z]
-    acts = jnp.concatenate([ref[:, :BLOCK] for ref in factors], axis=0)
-    pulled = jnp.concatenate([ref[:, 256:] for ref in factors], axis=0)
-    block = dot3(acts, pulled, TN)
+    wide = jnp.concatenate(
+        [
+            jnp.concatenate([ref[k * 2 * TXT : (k + 1) * 2 * TXT] for ref in factors], axis=0)
+            for k in range(FACTOR_ROWS // (2 * TXT))
+        ],
+        axis=1,
+    )
+    block = dot3(wide[:, :BLOCK], wide[:, 256:], TN)
     top = jnp.max(jnp.max(largest_ref[...], axis=0, keepdims=True), axis=1, keepdims=True)
     block_top = jnp.max(jnp.max(jnp.abs(block), axis=0, keepdims=True), axis=1, keepdims=True)
     power, block_power = power_of(top), power_of(block_top)
     scale = jnp.exp2(power)
     block = block * jnp.exp2(block_power)
-    powers = jnp.concatenate([jnp.broadcast_to(power, (8, 128)), jnp.broadcast_to(block_power, (8, 128))], axis=0)
+    powers = jnp.where(iota((8, 128), 0) < 4, power, block_power)
     for lab in range(N_LABEL):
+        first = lab * SENT_ROWS
         for j in range(PIECES):
-            start = AT_W_OUT + j * ROWS
-            out_ref[lab, start : start + ROWS] = block[lab * ROWS : (lab + 1) * ROWS, j * 128 : (j + 1) * 128]
-        out_ref[lab, AT_POWERS:AT_LABELS] = powers
-        out_ref[lab, AT_LABELS:] = labels_ref[lab]
+            start = first + AT_W_OUT + j * ROWS
+            out_ref[start : start + ROWS] = block[lab * ROWS : (lab + 1) * ROWS, j * 128 : (j + 1) * 128]
+        out_ref[first + AT_POWERS : first + AT_LABELS] = powers
+    for f in range(N_Z):
+        for g in range(N_LABEL // 8):
+            for k in range(SLOT_ROWS):
+                start = g * 8 * SENT_ROWS + AT_LABELS + f * SLOT_ROWS + k
+                row = FACTOR_ROWS + (g * SLOT_ROWS + k) * 8
+                out_ref[pl.ds(start, 8, stride=SENT_ROWS)] = factors[f][row : row + 8]
     for z in range(N_Z):
-
-        def place_rows(k, _):
+        for k in range(N_LABEL // 2):
             start = z * BLOCK + k * 2 * ROWS
-            rows = grad_ref[pl.ds(pl.multiple_of(start, 2 * ROWS), 2 * ROWS)] * scale
+            rows = grad_ref[start : start + 2 * ROWS] * scale
             for g in range(2):
                 for j in range(PIECES):
                     piece = rows[g * ROWS : (g + 1) * ROWS, j * 128 : (j + 1) * 128]
-                    first = z * CHUNK + j * ROWS
-                    out_ref[2 * k + g, first : first + ROWS] = piece
-            return 0
-
-        lax.fori_loop(0, N_LABEL // 2, place_rows, 0)
-
-
-def finish(grad, largest, label_rows, factors):
+                    first = (2 * k + g) * SENT_ROWS + z * CHUNK + j * ROWS
+                    out_ref[first : first + ROWS] = piece
+
+
+def finish(grad, largest, factors):
     return pl.pallas_call(
         finish_kernel,
-        out_shape=jax.ShapeDtypeStruct((N_LABEL, SENT_ROWS, 128), f32),
-        in_specs=vmem(3 + N_Z),
+        out_shape=jax.ShapeDtypeStruct((N_LABEL * SENT_ROWS, 128), f32),
+        in_specs=vmem(2 + N_Z),
         out_specs=pl.BlockSpec(memory_space=pltpu.VMEM),
         compiler_params=params(16),
         cost_estimate=cost(10**9, 5 * 10**6),
         name="finish_gradients",
-    )(grad, largest, label_rows, *factors)
+    )(grad, largest, *factors)
 
 
 def unpieced(rows):
     return jnp.concatenate([rows[j * ROWS : (j + 1) * ROWS] for j in range(PIECES)], axis=1)
 
 
-def middle_kernel(place_ref, came_ref, w_out_ref, *outs):
+def middle_kernel(place_ref, came_ref, w_out_ref, table_ref, *outs):
     total = jnp.zeros((AT_W_OUT, 128), f32)
     block = jnp.zeros((CHUNK, 128), f32)
-    vectors = []
     for lab in range(N_LABEL):
         total = total + came_ref[lab, :AT_W_OUT] * jnp.exp2(-came_ref[lab, AT_POWERS : AT_POWERS + 1])
-        block = block + came_ref[lab, AT_W_OUT:AT_POWERS] * jnp.exp2(-came_ref[lab, AT_POWERS + 8 : AT_POWERS + 9])
-        high = came_ref[lab, AT_LABELS : AT_LABELS + SLOT_ROWS]
-        low = came_ref[lab, AT_LABELS + SLOT_ROWS :]
-        vectors.append((high + low) * (1.0 / LABEL_SCALE))
+        block = block + came_ref[lab, AT_W_OUT:AT_POWERS] * jnp.exp2(-came_ref[lab, AT_POWERS + 4 : AT_POWERS + 5])
     w_out_ref[...] = unpieced(block)
-    vectors = jnp.concatenate(vectors, axis=0)
     for f in range(N_Z):
-        outs[f][CHUNK:] = vectors
+        z = lax.rem(place_ref[4] - f + N_Z, N_Z)
+        for lab in range(N_LABEL):
+            first = AT_LABELS + f * SLOT_ROWS
+            table_ref[z, lab * SLOT_ROWS : (lab + 1) * SLOT_ROWS] = came_ref[lab, first : first + SLOT_ROWS] * (
+                1.0 / LABEL_SCALE
+            )
     for z in range(N_Z):
         for f in range(N_Z):
 
             @pl.when(lax.rem(place_ref[4] + f, N_Z) == z)
             def _(z=z, f=f):
-                outs[f][:CHUNK] = total[z * CHUNK : (z + 1) * CHUNK]
+                outs[f][...] = total[z * CHUNK : (z + 1) * CHUNK]
 
 
 def middle(place, came):
     return pl.pallas_call(
         middle_kernel,
-        out_shape=(jax.ShapeDtypeStruct((ROWS, D), f32),)
-        + (jax.ShapeDtypeStruct((MOVED_ROWS, 128), f32),) * N_Z,
+        out_shape=(
+            jax.ShapeDtypeStruct((ROWS, D), f32),
+            jax.ShapeDtypeStruct((N_Z, N_LABEL * SLOT_ROWS, 128), f32),
+        )
+        + (jax.ShapeDtypeStruct((CHUNK, 128), f32),) * N_Z,
         in_specs=smem(1) + vmem(1),
-        out_specs=tuple(vmem(1 + N_Z)),
+        out_specs=tuple(vmem(2 + N_Z)),
         compiler_params=params(16),
         cost_estimate=cost(10**7, 4 * 10**6),
         name="plane_sums",
     )(place, came)
 
 
-def last_kernel(place_ref, *rest):
-    blocks, (w_in_ref, table_ref) = rest[:N_Z], rest[N_Z:]
-    total = blocks[0][:CHUNK]
-    for f in range(1, N_Z):
-        total = total + blocks[f][:CHUNK]
-    w_in_ref[...] = unpieced(total)
-    size = N_LABEL * SLOT_ROWS
-    for f in range(N_Z):
-        z = lax.rem(place_ref[4] - f + N_Z, N_Z)
-        table_ref[pl.ds(pl.multiple_of(z * size, size), size)] = blocks[f][CHUNK:]
-
-
-def last(place, blocks):
+def last_kernel(*rest):
+    blocks, w_in_ref = rest[:N_Z], rest[-1]
+    w_in_ref[...] = unpieced((blocks[0][...] + blocks[1][...]) + (blocks[2][...] + blocks[3][...]))
+
+
+def last(blocks, after):
     return pl.pallas_call(
         last_kernel,
-        out_shape=(
-            jax.ShapeDtypeStruct((ROWS, D), f32),
-            jax.ShapeDtypeStruct((N_CHIPS * SLOT_ROWS, 128), f32),
-        ),
-        in_specs=smem(1) + vmem(N_Z),
-        out_specs=tuple(vmem(2)),
+        out_shape=jax.ShapeDtypeStruct((ROWS, D), f32),
+        in_specs=vmem(N_Z) + [HBM],
+        out_specs=pl.BlockSpec(memory_space=pltpu.VMEM),
         compiler_params=params(8),
         cost_estimate=cost(10**6, 10**6),
         name="z_sums",
-    )(place, *blocks)
+    )(*blocks, in_hbm(after))
 
 
 def swap(value):
@@ -612,15 +631,17 @@
     slope, pooled, part, high, low = forward(place, both_lengths, gain_row, own, other, w_in_blocks, w_out_blocks)
     sums, label_rows = labels(owner_ids, part, swap(part), free_vectors)
 
-    free_grad = returned(owner_ids, slots)
-    back, *factors = pull(place, free_grad, swap(free_grad), sums, high, low, pooled)
+    free_grad, free_own = returned(owner_ids, slots)
+    back, *factors = pull(place, free_own, swap(free_own), sums, high, low, pooled, label_rows)
     factors = shift(factors, "z")
     grad, largest = backward(back, gain_row, own, other, slope)
-    sent_rows = finish(grad, largest, label_rows, factors)
+    sent_rows = finish(grad, largest, factors).reshape(N_LABEL, SENT_ROWS, 128)
     came = exchange(sent_rows.astype(jnp.float16), LABEL).astype(f32)
-    w_out_grad, *moved = middle(place, came)
-    w_in_grad, table = last(place, shift(moved, "z"))
+    w_out_grad, table, *moved = middle(place, came)
+    table = table.reshape(N_CHIPS * SLOT_ROWS, 128)
+    moved = shift(moved, "z")
     scores = slot_scores(place, names, queries, table, swap(table))
+    w_in_grad = last(moved, scores)
     return scores, free_grad, w_in_grad, w_out_grad
 
 

time: 107 us -> 95.9 us (0.90); the launches traced: 105 us -> 95.7 us
  local copies, waits for them, and re-layouts: 6.61 us -> 1.26 us
  waiting for transfers between devices: 8.8 us -> 3.72 us
  starting transfers between devices: 22 us -> 23.6 us
  Pallas kernels: 35.9 us -> 34.5 us
    unnamed x26 -> x14, local copies, waits for them, and re-layouts: 6.52 us -> 1.17 us
    ppermute x6, waiting for transfers between devices: 5.26 us -> 2.1 us  [shift(): lax.ppermute(blocks[k], axis, [(i, (i + k) % 4) for i in range(4)])]
    ppermute x6, waiting for transfers between devices: 3.55 us -> 1.62 us  [swap(): return lax.ppermute(value, 'core', ((0, 1), (1, 0)))]
    ppermute x6, starting transfers between devices: 9.17 us -> 10.6 us  [shift(): lax.ppermute(blocks[k], axis, [(i, (i + k) % 4) for i in range(4)])]
    pallas_call x1, Pallas kernels: 9.24 us -> 8.1 us  [backward(): pl.pallas_call(backward_kernel, out_shape=(shape((HALF, D), f32), shape((...]
  transfers between devices with their start and end apart: 13 -> 13, of which waited for: 5 -> 4; matrix products, arithmetic and copies ran while one was open for 1% -> 1% of each run, Pallas kernels for 26% -> 31%
where the time goes in v1:
time: 95.9 us; the launch traced here: 95.7 us
  Pallas kernels  34.5 us (36%)
  blocking collectives  30.3 us (32%)
  starting transfers between devices  23.6 us (25%)
  waiting for transfers between devices  3.72 us (4%)
  other arithmetic  1.48 us (2%)
  local copies, waits for them, and re-layouts  1.26 us (1%)
    all_to_all x1, blocking collectives, exchange(): return lax.all_to_all(value, axes, split_axis=0, concat_axis=0, tiled=True)  30.3 us
    pallas_call x1, Pallas kernels, forward(): pl.pallas_call(forward_kernel, out_shape=(pltpu.HBM((tokens, HALF), f32),...  13.6 us
    all_to_all x1, starting transfers between devices, exchange(): return lax.all_to_all(value, axes, split_axis=0, concat_axis=0, tiled=True)  11.7 us
    ppermute x6, starting transfers between devices, shift(): lax.ppermute(blocks[k], axis, [(i, (i + k) % 4) for i in range(4)])  10.6 us
    pallas_call x1, Pallas kernels, backward(): pl.pallas_call(backward_kernel, out_shape=(shape((HALF, D), f32), shape((...  8.1 us
    pallas_call x1, Pallas kernels, slot_partials(): pl.pallas_call(partial_kernel, out_shape=(shape, shape), in_specs=smem(1)...  3.24 us
    pallas_call x1, Pallas kernels, slot_scores(): pl.pallas_call(scores_kernel, out_shape=jax.ShapeDtypeStruct((QROWS, 2 *...  2.51 us
    ppermute x6, waiting for transfers between devices, shift(): lax.ppermute(blocks[k], axis, [(i, (i + k) % 4) for i in range(4)])  2.1 us
  transfers between devices with their start and end apart: 13, of which 4 were waited for; matrix products, arithmetic and copies ran while one was open for 1% of the time, Pallas kernels for 31%

profile of v1, /device:TPU:0, one launch (start us, length us, event | category | flops | bytes accessed | tf_op | source)
XLA Modules:
  0.0 95.7 jit_solution(10523399129780317394)
XLA Ops:
  0.6 0.0 copy-start.6
  0.6 0.0 copy-start.4
  0.7 0.1 collective-permute-start.3
  0.8 0.1 stack.23.place_ref
  0.8 3.2 %slot_partials.1 = (f32[1024,128]{1,0:T(8,128)S(1)}, f32[1024,128]{1,0:T(8,128)S(1)}) custom-call(s32[5]{0:T(128)S(1)} %stack.23.place_ref, s32[4,512]{1,0:T(4,128)} %bitcast.15, f32[512,256]{1,0:T(8,128)} %grad_ref.1, f32[512,768]{1,0:T(8,128)} %queries_ref.3), custom_call_target="tpu_custom_call" | custom-call | flops 603979776 | bytes 4000000 | tf_op jit(solution)/shard_map/slot_partials/pallas_call | solution.py:121
  4.1 0.6 collective-permute-start
  4.7 0.0 copy-done.6
  4.7 0.1 collective-permute-start.2
  4.8 0.0 copy-done.4
  4.8 1.4 %collective-permute-done.2 = s32[16]{0:T(128)S(1)} collective-permute-done((s32[16]{0:T(128)S(1)}, s32[16]{0:T(128)S(1)}, u32[]{:S(2)}, u32[]{:S(2)}) %collective-permute-start.2) | collective-permute-done | bytes 96 | tf_op jit(solution)/shard_map/ppermute | solution.py:604
  6.2 0.1 pad_add_fusion.lengths_ref
  6.3 0.0 collective-permute-done
  6.3 0.8 add.7
  7.1 11.7 %all-to-all-start = ((f32[64,16,128]{2,1,0:T(8,128)}), f32[64,16,128]{2,1,0:T(8,128)S(1)}, u32[]{:S(2)}, u32[]{:S(2)}) async-start(f32[64,16,128]{2,1,0:T(8,128)} %bitcast.7), calls=%async_computation | async-start | bytes 1048576 | tf_op jit(solution)/shard_map/all_to_all | solution.py:613
  18.8 0.0 collective-permute-done.3.other_ref
  18.8 0.0 copy-start.5
  18.8 1.1 %copy-done.5 = bf16[1024,768]{1,0:T(8,128)(2,1)} copy-done((bf16[1024,768]{1,0:T(8,128)(2,1)}, bf16[1024,768]{1,0:T(8,128)(2,1)S(1)}, u32[]{:S(2)}) %copy-start.5) | copy-done | bytes 1572888
  20.0 0.0 copy-start.3
  20.0 0.0 copy-start.1
  20.0 13.6 %encoder_forward.1 = (f32[2048,768]{1,0:T(8,128)}, f32[4,32,256]{2,1,0:T(8,128)S(1)}, f32[32,768]{1,0:T(8,128)S(1)}, bf16[4,192,768]{2,1,0:T(8,128)(2,1)S(1)}, bf16[4,192,768]{2,1,0:T(8,128)(2,1)S(1)}) custom-call(s32[5]{0:T(128)S(1)} %stack.23.place_ref, s32[32]{0:T(128)S(1)} %pad_add_fusion.lengths_ref, f32[1,768]{1,0:T(1,128)S(1)} %reshape.29.gain_ref, ...), custom_call_target="tpu_custom_call" | custom-call | flops 12079595520 | bytes 8000000 | tf_op jit(solution)/shard_map/encoder_forward/pallas_call | solution.py:249
  33.6 0.2 collective-permute-start.4
  33.8 0.0 all-to-all-done.came_ref
  33.8 0.0 copy-done.3
  33.8 1.3 %returned_gradients.1 = (f32[16,768]{1,0:T(8,128)}, f32[16,768]{1,0:T(8,128)S(1)}) custom-call(s32[16]{0:T(128)S(1)} %bitcast.17, f32[64,16,128]{2,1,0:T(8,128)S(1)} %all-to-all-done.came_ref), custom_call_target="tpu_custom_call" | custom-call | flops 100000 | bytes 500000 | tf_op jit(solution)/shard_map/returned_gradients/pallas_call | solution.py:380
  35.0 0.4 collective-permute-start.1
  35.5 0.0 collective-permute-done.4.came_ref
  35.5 0.0 copy-done.1
  35.5 0.7 label_vectors.1
  36.2 0.2 collective-permute-done.1.free_other_ref
  36.4 1.8 %pull_back.1 = (f32[32,768]{1,0:T(8,128)S(1)}, f32[448,128]{1,0:T(8,128)S(1)}, f32[448,128]{1,0:T(8,128)S(1)}, f32[448,128]{1,0:T(8,128)S(1)}, f32[448,128]{1,0:T(8,128)S(1)}) custom-call(s32[5]{0:T(128)S(1)} %stack.23.place_ref, f32[16,768]{1,0:T(8,128)S(1)} %get-tuple-element.30.free_own_ref, f32[16,768]{1,0:T(8,128)S(1)} %collective-permute-done.1.free_other_ref, ...), custom_call_target="tpu_custom_call" | custom-call | flops 113246208 | bytes 3000000 | tf_op jit(solution)/shard_map/pull_back/pallas_call | solution.py:415
  38.2 1.5 %collective-permute-start.5 = (f32[448,128]{1,0:T(8,128)S(1)}, f32[448,128]{1,0:T(8,128)S(1)}, u32[]{:S(2)}, u32[]{:S(2)}) collective-permute-start(f32[448,128]{1,0:T(8,128)S(1)} %get-tuple-element.42), channel_id=1, source_target_pairs={{0,32},{32,64},{64,96},{96,0},{1,33},{33,65},{65,97},{97,1},{2,34}... | collective-permute-start | bytes 688136 | tf_op jit(solution)/shard_map/ppermute | solution.py:608
  39.7 2.9 %collective-permute-start.6 = (f32[448,128]{1,0:T(8,128)S(1)}, f32[448,128]{1,0:T(8,128)S(1)}, u32[]{:S(2)}, u32[]{:S(2)}) collective-permute-start(f32[448,128]{1,0:T(8,128)S(1)} %get-tuple-element.43), channel_id=1, source_target_pairs={{0,64},{32,96},{64,0},{96,32},{1,65},{33,97},{65,1},{97,33},{2,66}... | collective-permute-start | bytes 688136 | tf_op jit(solution)/shard_map/ppermute | solution.py:608
  42.5 1.4 %collective-permute-start.7 = (f32[448,128]{1,0:T(8,128)S(1)}, f32[448,128]{1,0:T(8,128)S(1)}, u32[]{:S(2)}, u32[]{:S(2)}) collective-permute-start(f32[448,128]{1,0:T(8,128)S(1)} %get-tuple-element.44), channel_id=1, source_target_pairs={{0,96},{32,0},{64,32},{96,64},{1,97},{33,1},{65,33},{97,65},{2,98}... | collective-permute-start | bytes 688136 | tf_op jit(solution)/shard_map/ppermute | solution.py:608
  43.9 8.1 %encoder_backward.1 = (f32[768,768]{1,0:T(8,128)S(1)}, f32[3,768]{1,0:T(4,128)S(1)}) custom-call(f32[32,768]{1,0:T(8,128)S(1)} %get-tuple-element.37.back_ref, f32[1,768]{1,0:T(1,128)S(1)} %reshape.29.gain_ref, bf16[1024,768]{1,0:T(8,128)(2,1)} %bitcast.24, bf16[1024,768]{1,0:T(8,128)(2,1)} %copy-done.5, f32[2048,768]{1,0:T(8,128)} %get-tuple-element.38.slope_ref), custom_call_target="tpu_custom_call" | custom-call | flops 6039797760 | bytes 4000000 | tf_op jit(solution)/shard_map/encoder_backward/pallas_call | solution.py:473
  52.0 0.0 collective-permute-done.5.rest_1_
  52.0 1.3 %collective-permute-done.6.rest_2_ = f32[448,128]{1,0:T(8,128)S(1)} collective-permute-done((f32[448,128]{1,0:T(8,128)S(1)}, f32[448,128]{1,0:T(8,128)S(1)}, u32[]{:S(2)}, u32[]{:S(2)}) %collective-permute-start.6) | collective-permute-done | bytes 229408 | tf_op jit(solution)/shard_map/ppermute | solution.py:608
  53.3 0.0 collective-permute-done.7.rest_3_
  53.3 0.9 finish_gradients.1
  54.2 0.2 convert_element_type.9
  54.4 30.3 %all_to_all.10 = f16[16,416,128]{2,1,0:T(8,128)(2,1)S(1)} all-to-all(f16[16,416,128]{2,1,0:T(8,128)(2,1)S(1)} %bitcast.19), channel_id=1, replica_groups=mesh['z'=4,'core'=2,'x'=4,'y'=4] {'x','y'}, dimensions={0} | all-to-all | bytes 3407872 | tf_op jit(solution)/shard_map/all_to_all | solution.py:613
  84.7 0.3 convert_element_type.11.came_ref
  85.1 0.0 copy-start
  85.1 0.0 copy-start.2
  85.1 1.7 %plane_sums.1 = (f32[12,768]{1,0:T(8,128)}, f32[4,192,128]{2,1,0:T(8,128)S(1)}, f32[72,128]{1,0:T(8,128)S(1)}, f32[72,128]{1,0:T(8,128)S(1)}, f32[72,128]{1,0:T(8,128)S(1)}, /*index=5*/f32[72,128]{1,0:T(8,128)S(1)}) custom-call(s32[5]{0:T(128)S(1)} %stack.23.place_ref, f32[16,416,128]{2,1,0:T(8,128)S(1)} %convert_element_type.11.came_ref), custom_call_target="tpu_custom_call" | custom-call | flops 10000000 | bytes 4000000 | tf_op jit(solution)/shard_map/plane_sums/pallas_call | solution.py:571
  86.8 0.0 collective-permute-start.8
  86.8 1.0 %collective-permute-start.9 = (f32[72,128]{1,0:T(8,128)S(1)}, f32[72,128]{1,0:T(8,128)S(1)}, u32[]{:S(2)}, u32[]{:S(2)}) collective-permute-start(f32[72,128]{1,0:T(8,128)S(1)} %get-tuple-element.48), channel_id=1, source_target_pairs={{0,32},{32,64},{64,96},{96,0},{1,33},{33,65},{65,97},{97,1},{2,34}... | collective-permute-start | bytes 110600 | tf_op jit(solution)/shard_map/ppermute | solution.py:608
  87.8 3.3 %collective-permute-start.10 = (f32[72,128]{1,0:T(8,128)S(1)}, f32[72,128]{1,0:T(8,128)S(1)}, u32[]{:S(2)}, u32[]{:S(2)}) collective-permute-start(f32[72,128]{1,0:T(8,128)S(1)} %get-tuple-element.49), channel_id=1, source_target_pairs={{0,64},{32,96},{64,0},{96,32},{1,65},{33,97},{65,1},{97,33},{2,66}... | collective-permute-start | bytes 110600 | tf_op jit(solution)/shard_map/ppermute | solution.py:608
  91.1 0.6 collective-permute-start.11
  91.7 0.0 collective-permute-done.8.other_ref
  91.7 0.0 copy-done
  91.7 0.0 copy-done.2
  91.7 2.5 %slot_scores.1.rest_4_ = f32[512,256]{1,0:T(8,128)} custom-call(s32[5]{0:T(128)S(1)} %stack.23.place_ref, s32[4,512]{1,0:T(4,128)S(1)} %bitcast.16, f32[512,768]{1,0:T(8,128)S(1)} %copy-done, f32[768,128]{1,0:T(8,128)S(1)} %bitcast.14, f32[768,128]{1,0:T(8,128)S(1)} %collective-permute-done.8.other_ref), custom_call_target="tpu_custom_call" | custom-call | flops 603979776 | bytes 4000000 | tf_op jit(solution)/shard_map/slot_scores/pallas_call | solution.py:355
  94.2 0.0 collective-permute-done.9.rest_1_
  94.2 0.0 collective-permute-done.10.rest_2_
  94.2 0.8 collective-permute-done.11.rest_3_
  95.0 0.6 z_sums.1
  (1 shorter events, 0.0 us)
Async XLA Ops:
  0.6 4.0 %copy-start.6 = (s32[16]{0:T(128)S(1)}, s32[16]{0:T(128)}, u32[]{:S(2)}) copy-start(s32[16]{0:T(128)} %param.11) | copy-start | bytes 196
  0.6 4.1 %copy-start.4 = (f32[768]{0:T(1024)S(1)}, f32[768]{0:T(1024)}, u32[]{:S(2)}) copy-start(f32[768]{0:T(1024)} %param.13) | copy-start | bytes 9220
  0.7 18.2 %collective-permute-start.3 = (bf16[1024,768]{1,0:T(8,128)(2,1)}, bf16[1024,768]{1,0:T(8,128)(2,1)S(1)}, u32[]{:S(2)}, u32[]{:S(2)}) collective-permute-start(bf16[1024,768]{1,0:T(8,128)(2,1)} %bitcast.22), channel_id=1, source_target_pairs={{0,16},{16,0},{1,17},{17,1},{2,18},{18,2},{3,19},{19,3},{4,20},{20... | collective-permute-start | bytes 4718600 | tf_op jit(solution)/shard_map/ppermute | solution.py:604
  4.1 2.2 %collective-permute-start = (f32[1024,128]{1,0:T(8,128)S(1)}, f32[1024,128]{1,0:T(8,128)S(1)}, u32[]{:S(2)}, u32[]{:S(2)}) collective-permute-start(f32[1024,128]{1,0:T(8,128)S(1)} %get-tuple-element.29), channel_id=1, source_target_pairs={{0,16},{16,0},{1,17},{17,1},{2,18},{18,2},{3,19},{19,3},{4,20},{20... | collective-permute-start | bytes 1572872 | tf_op jit(solution)/shard_map/ppermute | solution.py:604
  4.7 1.5 %collective-permute-start.2 = (s32[16]{0:T(128)S(1)}, s32[16]{0:T(128)S(1)}, u32[]{:S(2)}, u32[]{:S(2)}) collective-permute-start(s32[16]{0:T(128)S(1)} %copy-done.6), channel_id=1, source_target_pairs={{0,16},{16,0},{1,17},{17,1},{2,18},{18,2},{3,19},{19,3},{4,20},{20... | collective-permute-start | bytes 200 | tf_op jit(solution)/shard_map/ppermute | solution.py:604
  7.1 26.7 %all-to-all-start = ((f32[64,16,128]{2,1,0:T(8,128)}), f32[64,16,128]{2,1,0:T(8,128)S(1)}, u32[]{:S(2)}, u32[]{:S(2)}) async-start(f32[64,16,128]{2,1,0:T(8,128)} %bitcast.7), calls=%async_computation | async-start | bytes 1048576 | tf_op jit(solution)/shard_map/all_to_all | solution.py:613
  18.8 1.1 %copy-start.5 = (bf16[1024,768]{1,0:T(8,128)(2,1)}, bf16[1024,768]{1,0:T(8,128)(2,1)S(1)}, u32[]{:S(2)}) copy-start(bf16[1024,768]{1,0:T(8,128)(2,1)S(1)} %collective-permute-done.3.other_ref) | copy-start | bytes 4718596
  20.0 13.8 %copy-start.3 = (s32[16,1]{0,1:T(1,128)S(1)}, s32[16,1]{0,1:T(1,128)}, u32[]{:S(2)}) copy-start(s32[16,1]{0,1:T(1,128)} %param.12) | copy-start | bytes 196
  20.0 15.5 %copy-start.1 = (f32[16,768]{1,0:T(8,128)S(1)}, f32[16,768]{1,0:T(8,128)}, u32[]{:S(2)}) copy-start(f32[16,768]{1,0:T(8,128)} %free_ref.1) | copy-start | bytes 147460
  33.6 1.9 %collective-permute-start.4 = (f32[32,768]{1,0:T(8,128)S(1)}, f32[32,768]{1,0:T(8,128)S(1)}, u32[]{:S(2)}, u32[]{:S(2)}) collective-permute-start(f32[32,768]{1,0:T(8,128)S(1)} %get-tuple-element.31.part_ref), channel_id=1, source_target_pairs={{0,16},{16,0},{1,17},{17,1},{2,18},{18,2},{3,19},{19,3},{4,20},{20... | collective-permute-start | bytes 294920 | tf_op jit(solution)/shard_map/ppermute | solution.py:604
  35.0 1.3 %collective-permute-start.1 = (f32[16,768]{1,0:T(8,128)S(1)}, f32[16,768]{1,0:T(8,128)S(1)}, u32[]{:S(2)}, u32[]{:S(2)}) collective-permute-start(f32[16,768]{1,0:T(8,128)S(1)} %get-tuple-element.30.free_own_ref), channel_id=1, source_target_pairs={{0,16},{16,0},{1,17},{17,1},{2,18},{18,2},{3,19},{19,3},{4,20},{20... | collective-permute-start | bytes 147464 | tf_op jit(solution)/shard_map/ppermute | solution.py:604
  38.2 13.8 %collective-permute-start.5 = (f32[448,128]{1,0:T(8,128)S(1)}, f32[448,128]{1,0:T(8,128)S(1)}, u32[]{:S(2)}, u32[]{:S(2)}) collective-permute-start(f32[448,128]{1,0:T(8,128)S(1)} %get-tuple-element.42), channel_id=1, source_target_pairs={{0,32},{32,64},{64,96},{96,0},{1,33},{33,65},{65,97},{97,1},{2,34}... | collective-permute-start | bytes 688136 | tf_op jit(solution)/shard_map/ppermute | solution.py:608
  39.7 13.6 %collective-permute-start.6 = (f32[448,128]{1,0:T(8,128)S(1)}, f32[448,128]{1,0:T(8,128)S(1)}, u32[]{:S(2)}, u32[]{:S(2)}) collective-permute-start(f32[448,128]{1,0:T(8,128)S(1)} %get-tuple-element.43), channel_id=1, source_target_pairs={{0,64},{32,96},{64,0},{96,32},{1,65},{33,97},{65,1},{97,33},{2,66}... | collective-permute-start | bytes 688136 | tf_op jit(solution)/shard_map/ppermute | solution.py:608
  42.5 10.8 %collective-permute-start.7 = (f32[448,128]{1,0:T(8,128)S(1)}, f32[448,128]{1,0:T(8,128)S(1)}, u32[]{:S(2)}, u32[]{:S(2)}) collective-permute-start(f32[448,128]{1,0:T(8,128)S(1)} %get-tuple-element.44), channel_id=1, source_target_pairs={{0,96},{32,0},{64,32},{96,64},{1,97},{33,1},{65,33},{97,65},{2,98}... | collective-permute-start | bytes 688136 | tf_op jit(solution)/shard_map/ppermute | solution.py:608
  85.1 6.6 %copy-start = (f32[512,768]{1,0:T(8,128)S(1)}, f32[512,768]{1,0:T(8,128)}, u32[]{:S(2)}) copy-start(f32[512,768]{1,0:T(8,128)} %queries_ref.3) | copy-start | bytes 4718596
  85.1 6.6 %copy-start.2 = (s32[512,4]{0,1:T(4,128)S(1)}, s32[512,4]{0,1:T(4,128)}, u32[]{:S(2)}) copy-start(s32[512,4]{0,1:T(4,128)} %param.18) | copy-start | bytes 24580
  86.8 4.9 %collective-permute-start.8 = (f32[768,128]{1,0:T(8,128)S(1)}, f32[768,128]{1,0:T(8,128)S(1)}, u32[]{:S(2)}, u32[]{:S(2)}) collective-permute-start(f32[768,128]{1,0:T(8,128)S(1)} %bitcast.13), channel_id=1, source_target_pairs={{0,16},{16,0},{1,17},{17,1},{2,18},{18,2},{3,19},{19,3},{4,20},{20... | collective-permute-start | bytes 1179656 | tf_op jit(solution)/shard_map/ppermute | solution.py:604
  86.8 7.4 %collective-permute-start.9 = (f32[72,128]{1,0:T(8,128)S(1)}, f32[72,128]{1,0:T(8,128)S(1)}, u32[]{:S(2)}, u32[]{:S(2)}) collective-permute-start(f32[72,128]{1,0:T(8,128)S(1)} %get-tuple-element.48), channel_id=1, source_target_pairs={{0,32},{32,64},{64,96},{96,0},{1,33},{33,65},{65,97},{97,1},{2,34}... | collective-permute-start | bytes 110600 | tf_op jit(solution)/shard_map/ppermute | solution.py:608
  87.8 6.4 %collective-permute-start.10 = (f32[72,128]{1,0:T(8,128)S(1)}, f32[72,128]{1,0:T(8,128)S(1)}, u32[]{:S(2)}, u32[]{:S(2)}) collective-permute-start(f32[72,128]{1,0:T(8,128)S(1)} %get-tuple-element.49), channel_id=1, source_target_pairs={{0,64},{32,96},{64,0},{96,32},{1,65},{33,97},{65,1},{97,33},{2,66}... | collective-permute-start | bytes 110600 | tf_op jit(solution)/shard_map/ppermute | solution.py:608
  91.1 4.0 %collective-permute-start.11 = (f32[72,128]{1,0:T(8,128)S(1)}, f32[72,128]{1,0:T(8,128)S(1)}, u32[]{:S(2)}, u32[]{:S(2)}) collective-permute-start(f32[72,128]{1,0:T(8,128)S(1)} %get-tuple-element.50), channel_id=1, source_target_pairs={{0,96},{32,0},{64,32},{96,64},{1,97},{33,1},{65,33},{97,65},{2,98}... | collective-permute-start | bytes 110600 | tf_op jit(solution)/shard_map/ppermute | solution.py:608

commit v2 on v1

--- a/solution.py
+++ b/solution.py
@@ -389,13 +389,36 @@
     )(owners, came)
 
 
-def pull_kernel(place_ref, free_own_ref, free_other_ref, sums_ref, high_ref, low_ref, pooled_ref, labels_ref, back_ref, *outs):
+def pull_kernel(place_ref, free_own_ref, free_other_ref, sums_ref, pooled_ref, labels_ref, pulled_ref, *outs):
     free = jnp.concatenate([free_own_ref[...], free_other_ref[...]], axis=0)
     sums = sums_ref[...]
     unit = unit_rows(sums)
     along = jnp.sum(sums * free, axis=-1, keepdims=True)
     pulled = unit * free - (unit * unit * unit * along) * sums
-    p_high, p_low = split(pulled)
+    pulled_ref[...] = pulled
+    for f in range(N_Z):
+        acts = pooled_ref[lax.rem(place_ref[4] + f, N_Z)]
+        for k in range(FACTOR_ROWS // (2 * TXT)):
+            piece = acts[:, k * 128 : (k + 1) * 128] if k < 2 else pulled[:, (k - 2) * 128 : (k - 1) * 128]
+            outs[f][k * 2 * TXT : (k + 1) * 2 * TXT] = piece
+        outs[f][FACTOR_ROWS:] = labels_ref[...]
+
+
+def pull(place, free_own, free_other, sums, pooled, label_rows):
+    return pl.pallas_call(
+        pull_kernel,
+        out_shape=(jax.ShapeDtypeStruct((2 * TXT, HALF), f32),)
+        + (jax.ShapeDtypeStruct((MOVED_ROWS, 128), f32),) * N_Z,
+        in_specs=smem(1) + vmem(5),
+        out_specs=tuple(vmem(1 + N_Z)),
+        compiler_params=params(12),
+        cost_estimate=cost(6 * 32 * HALF * D, 3 * 10**6),
+        name="pull_back",
+    )(place, free_own, free_other, sums, pooled, label_rows)
+
+
+def w_out_kernel(pulled_ref, high_ref, low_ref, back_ref):
+    p_high, p_low = split(pulled_ref[...])
     back_ref[...] = jnp.concatenate(
         [
             dot(p_high, high_ref[z], NT) + (dot(p_high, low_ref[z], NT) + dot(p_low, high_ref[z], NT))
@@ -403,25 +426,18 @@
         ],
         axis=1,
     )
-    for f in range(N_Z):
-        acts = pooled_ref[lax.rem(place_ref[4] + f, N_Z)]
-        for k in range(FACTOR_ROWS // (2 * TXT)):
-            piece = acts[:, k * 128 : (k + 1) * 128] if k < 2 else pulled[:, (k - 2) * 128 : (k - 1) * 128]
-            outs[f][k * 2 * TXT : (k + 1) * 2 * TXT] = piece
-        outs[f][FACTOR_ROWS:] = labels_ref[...]
-
-
-def pull(place, free_own, free_other, sums, high, low, pooled, label_rows):
-    return pl.pallas_call(
-        pull_kernel,
-        out_shape=(jax.ShapeDtypeStruct((2 * TXT, HALF), f32),)
-        + (jax.ShapeDtypeStruct((MOVED_ROWS, 128), f32),) * N_Z,
-        in_specs=smem(1) + vmem(7),
-        out_specs=tuple(vmem(1 + N_Z)),
+
+
+def through_w_out(pulled, high, low):
+    return pl.pallas_call(
+        w_out_kernel,
+        out_shape=jax.ShapeDtypeStruct((2 * TXT, HALF), f32),
+        in_specs=vmem(3),
+        out_specs=pl.BlockSpec(memory_space=pltpu.VMEM),
         compiler_params=params(12),
         cost_estimate=cost(6 * 32 * HALF * D, 3 * 10**6),
-        name="pull_back",
-    )(place, free_own, free_other, sums, high, low, pooled, label_rows)
+        name="back_through_w_out",
+    )(pulled, high, low)
 
 
 def backward_kernel(back_ref, gain_ref, own_ref, other_ref, slope_ref, grad, largest, x_buf, slope_buf, sem):
@@ -632,7 +648,8 @@
     sums, label_rows = labels(owner_ids, part, swap(part), free_vectors)
 
     free_grad, free_own = returned(owner_ids, slots)
-    back, *factors = pull(place, free_own, swap(free_own), sums, high, low, pooled, label_rows)
+    pulled, *factors = pull(place, free_own, swap(free_own), sums, pooled, label_rows)
+    back = through_w_out(pulled, high, low)
     factors = shift(factors, "z")
     grad, largest = backward(back, gain_row, own, other, slope)
     sent_rows = finish(grad, largest, factors).reshape(N_LABEL, SENT_ROWS, 128)

time: 95.9 us -> 94.8 us (0.989)
  waiting for transfers between devices: 3.72 us -> 2.45 us
    ppermute x6, waiting for transfers between devices: 2.1 us -> 0.83 us  [shift(): lax.ppermute(blocks[k], axis, [(i, (i + k) % 4) for i in range(4)])]
    pallas_call x0 -> x1, Pallas kernels: none -> 1.22 us  [through_w_out(): pl.pallas_call(w_out_kernel, out_shape=jax.ShapeDtypeStruct((2 * TXT, HAL...]
    pallas_call x1, Pallas kernels: 1.84 us -> 0.67 us  [pull(): pl.pallas_call(pull_kernel, out_shape=(jax.ShapeDtypeStruct((2 * TXT, HAL...]
  transfers between devices with their start and end apart: 13 -> 13, of which waited for: 4 -> 3; matrix products, arithmetic and copies ran while one was open for 1% -> 1% of each run, Pallas kernels for 31% -> 32%
where the time goes in v2:
time: 94.8 us; the launch traced here: 94.5 us
  Pallas kernels  34.6 us (36%)
  blocking collectives  30.3 us (32%)
  starting transfers between devices  23.6 us (25%)
  waiting for transfers between devices  2.45 us (3%)
  other arithmetic  1.48 us (2%)
  local copies, waits for them, and re-layouts  1.26 us (1%)
    all_to_all x1, blocking collectives, exchange(): return lax.all_to_all(value, axes, split_axis=0, concat_axis=0, tiled=True)  30.3 us
    pallas_call x1, Pallas kernels, forward(): pl.pallas_call(forward_kernel, out_shape=(pltpu.HBM((tokens, HALF), f32),...  13.6 us
    all_to_all x1, starting transfers between devices, exchange(): return lax.all_to_all(value, axes, split_axis=0, concat_axis=0, tiled=True)  11.7 us
    ppermute x6, starting transfers between devices, shift(): lax.ppermute(blocks[k], axis, [(i, (i + k) % 4) for i in range(4)])  10.6 us
    pallas_call x1, Pallas kernels, backward(): pl.pallas_call(backward_kernel, out_shape=(shape((HALF, D), f32), shape((...  8.14 us
    pallas_call x1, Pallas kernels, slot_partials(): pl.pallas_call(partial_kernel, out_shape=(shape, shape), in_specs=smem(1)...  3.24 us
    pallas_call x1, Pallas kernels, slot_scores(): pl.pallas_call(scores_kernel, out_shape=jax.ShapeDtypeStruct((QROWS, 2 *...  2.52 us
  transfers between devices with their start and end apart: 13, of which 3 were waited for; matrix products, arithmetic and copies ran while one was open for 1% of the time, Pallas kernels for 32%

profile of v2, /device:TPU:0, one launch (start us, length us, event | category | flops | bytes accessed | tf_op | source)
XLA Modules:
  0.0 94.5 jit_solution(9222473073063883952)
XLA Ops:
  0.6 0.0 copy-start.6
  0.6 0.0 copy-start.4
  0.7 0.1 collective-permute-start.3
  0.8 0.1 stack.23.place_ref
  0.8 3.2 %slot_partials.1 = (f32[1024,128]{1,0:T(8,128)S(1)}, f32[1024,128]{1,0:T(8,128)S(1)}) custom-call(s32[5]{0:T(128)S(1)} %stack.23.place_ref, s32[4,512]{1,0:T(4,128)} %bitcast.15, f32[512,256]{1,0:T(8,128)} %grad_ref.1, f32[512,768]{1,0:T(8,128)} %queries_ref.3), custom_call_target="tpu_custom_call" | custom-call | flops 603979776 | bytes 4000000 | tf_op jit(solution)/shard_map/slot_partials/pallas_call | solution.py:121
  4.1 0.6 collective-permute-start
  4.7 0.0 copy-done.6
  4.7 0.1 collective-permute-start.2
  4.8 0.0 copy-done.4
  4.8 1.4 %collective-permute-done.2 = s32[16]{0:T(128)S(1)} collective-permute-done((s32[16]{0:T(128)S(1)}, s32[16]{0:T(128)S(1)}, u32[]{:S(2)}, u32[]{:S(2)}) %collective-permute-start.2) | collective-permute-done | bytes 96 | tf_op jit(solution)/shard_map/ppermute | solution.py:620
  6.2 0.1 pad_add_fusion.lengths_ref
  6.3 0.0 collective-permute-done
  6.3 0.8 add.7
  7.1 11.7 %all-to-all-start = ((f32[64,16,128]{2,1,0:T(8,128)}), f32[64,16,128]{2,1,0:T(8,128)S(1)}, u32[]{:S(2)}, u32[]{:S(2)}) async-start(f32[64,16,128]{2,1,0:T(8,128)} %bitcast.7), calls=%async_computation | async-start | bytes 1048576 | tf_op jit(solution)/shard_map/all_to_all | solution.py:629
  18.8 0.0 collective-permute-done.3.other_ref
  18.8 0.0 copy-start.5
  18.8 1.1 %copy-done.5 = bf16[1024,768]{1,0:T(8,128)(2,1)} copy-done((bf16[1024,768]{1,0:T(8,128)(2,1)}, bf16[1024,768]{1,0:T(8,128)(2,1)S(1)}, u32[]{:S(2)}) %copy-start.5) | copy-done | bytes 1572888
  20.0 0.0 copy-start.3
  20.0 0.0 copy-start.1
  20.0 13.6 %encoder_forward.1 = (f32[2048,768]{1,0:T(8,128)}, f32[4,32,256]{2,1,0:T(8,128)S(1)}, f32[32,768]{1,0:T(8,128)S(1)}, bf16[4,192,768]{2,1,0:T(8,128)(2,1)S(1)}, bf16[4,192,768]{2,1,0:T(8,128)(2,1)S(1)}) custom-call(s32[5]{0:T(128)S(1)} %stack.23.place_ref, s32[32]{0:T(128)S(1)} %pad_add_fusion.lengths_ref, f32[1,768]{1,0:T(1,128)S(1)} %reshape.29.gain_ref, ...), custom_call_target="tpu_custom_call" | custom-call | flops 12079595520 | bytes 8000000 | tf_op jit(solution)/shard_map/encoder_forward/pallas_call | solution.py:249
  33.6 0.2 collective-permute-start.4
  33.8 0.0 all-to-all-done.came_ref
  33.8 0.0 copy-done.3
  33.8 1.3 %returned_gradients.1 = (f32[16,768]{1,0:T(8,128)}, f32[16,768]{1,0:T(8,128)S(1)}) custom-call(s32[16]{0:T(128)S(1)} %bitcast.17, f32[64,16,128]{2,1,0:T(8,128)S(1)} %all-to-all-done.came_ref), custom_call_target="tpu_custom_call" | custom-call | flops 100000 | bytes 500000 | tf_op jit(solution)/shard_map/returned_gradients/pallas_call | solution.py:380
  35.0 0.4 collective-permute-start.1
  35.5 0.0 collective-permute-done.4.came_ref
  35.5 0.0 copy-done.1
  35.5 0.7 label_vectors.1
  36.2 0.2 collective-permute-done.1.free_other_ref
  36.4 0.7 pull_back.1
  37.0 1.5 %collective-permute-start.5 = (f32[448,128]{1,0:T(8,128)S(1)}, f32[448,128]{1,0:T(8,128)S(1)}, u32[]{:S(2)}, u32[]{:S(2)}) collective-permute-start(f32[448,128]{1,0:T(8,128)S(1)} %get-tuple-element.42), channel_id=1, source_target_pairs={{0,32},{32,64},{64,96},{96,0},{1,33},{33,65},{65,97},{97,1},{2,34}... | collective-permute-start | bytes 688136 | tf_op jit(solution)/shard_map/ppermute | solution.py:624
  38.5 2.9 %collective-permute-start.6 = (f32[448,128]{1,0:T(8,128)S(1)}, f32[448,128]{1,0:T(8,128)S(1)}, u32[]{:S(2)}, u32[]{:S(2)}) collective-permute-start(f32[448,128]{1,0:T(8,128)S(1)} %get-tuple-element.43), channel_id=1, source_target_pairs={{0,64},{32,96},{64,0},{96,32},{1,65},{33,97},{65,1},{97,33},{2,66}... | collective-permute-start | bytes 688136 | tf_op jit(solution)/shard_map/ppermute | solution.py:624
  41.4 1.4 %collective-permute-start.7 = (f32[448,128]{1,0:T(8,128)S(1)}, f32[448,128]{1,0:T(8,128)S(1)}, u32[]{:S(2)}, u32[]{:S(2)}) collective-permute-start(f32[448,128]{1,0:T(8,128)S(1)} %get-tuple-element.44), channel_id=1, source_target_pairs={{0,96},{32,0},{64,32},{96,64},{1,97},{33,1},{65,33},{97,65},{2,98}... | collective-permute-start | bytes 688136 | tf_op jit(solution)/shard_map/ppermute | solution.py:624
  42.7 1.2 %back_through_w_out.1.back_ref = f32[32,768]{1,0:T(8,128)S(1)} custom-call(f32[32,768]{1,0:T(8,128)S(1)} %get-tuple-element.35.pulled_ref, bf16[4,192,768]{2,1,0:T(8,128)(2,1)S(1)} %get-tuple-element.36.high_ref, bf16[4,192,768]{2,1,0:T(8,128)(2,1)S(1)} %get-tuple-element.37.low_ref), custom_call_target="tpu_custom_call" | custom-call | flops 113246208 | bytes 3000000 | tf_op jit(solution)/shard_map/back_through_w_out/pallas_call | solution.py:432
  44.0 8.1 %encoder_backward.1 = (f32[768,768]{1,0:T(8,128)S(1)}, f32[3,768]{1,0:T(4,128)S(1)}) custom-call(f32[32,768]{1,0:T(8,128)S(1)} %back_through_w_out.1.back_ref, f32[1,768]{1,0:T(1,128)S(1)} %reshape.29.gain_ref, bf16[1024,768]{1,0:T(8,128)(2,1)} %bitcast.24, bf16[1024,768]{1,0:T(8,128)(2,1)} %copy-done.5, f32[2048,768]{1,0:T(8,128)} %get-tuple-element.38.slope_ref), custom_call_target="tpu_custom_call" | custom-call | flops 6039797760 | bytes 4000000 | tf_op jit(solution)/shard_map/encoder_backward/pallas_call | solution.py:489
  52.1 0.0 collective-permute-done.5.rest_1_
  52.1 0.0 collective-permute-done.6.rest_2_
  52.1 0.0 collective-permute-done.7.rest_3_
  52.1 0.9 finish_gradients.1
  53.1 0.2 convert_element_type.9
  53.3 30.3 %all_to_all.10 = f16[16,416,128]{2,1,0:T(8,128)(2,1)S(1)} all-to-all(f16[16,416,128]{2,1,0:T(8,128)(2,1)S(1)} %bitcast.19), channel_id=1, replica_groups=mesh['z'=4,'core'=2,'x'=4,'y'=4] {'x','y'}, dimensions={0} | all-to-all | bytes 3407872 | tf_op jit(solution)/shard_map/all_to_all | solution.py:629
  83.6 0.3 convert_element_type.11.came_ref
  83.9 0.0 copy-start
  83.9 0.0 copy-start.2
  84.0 1.7 %plane_sums.1 = (f32[12,768]{1,0:T(8,128)}, f32[4,192,128]{2,1,0:T(8,128)S(1)}, f32[72,128]{1,0:T(8,128)S(1)}, f32[72,128]{1,0:T(8,128)S(1)}, f32[72,128]{1,0:T(8,128)S(1)}, /*index=5*/f32[72,128]{1,0:T(8,128)S(1)}) custom-call(s32[5]{0:T(128)S(1)} %stack.23.place_ref, f32[16,416,128]{2,1,0:T(8,128)S(1)} %convert_element_type.11.came_ref), custom_call_target="tpu_custom_call" | custom-call | flops 10000000 | bytes 4000000 | tf_op jit(solution)/shard_map/plane_sums/pallas_call | solution.py:587
  85.6 0.0 collective-permute-start.8
  85.6 1.0 %collective-permute-start.9 = (f32[72,128]{1,0:T(8,128)S(1)}, f32[72,128]{1,0:T(8,128)S(1)}, u32[]{:S(2)}, u32[]{:S(2)}) collective-permute-start(f32[72,128]{1,0:T(8,128)S(1)} %get-tuple-element.48), channel_id=1, source_target_pairs={{0,32},{32,64},{64,96},{96,0},{1,33},{33,65},{65,97},{97,1},{2,34}... | collective-permute-start | bytes 110600 | tf_op jit(solution)/shard_map/ppermute | solution.py:624
  86.6 3.3 %collective-permute-start.10 = (f32[72,128]{1,0:T(8,128)S(1)}, f32[72,128]{1,0:T(8,128)S(1)}, u32[]{:S(2)}, u32[]{:S(2)}) collective-permute-start(f32[72,128]{1,0:T(8,128)S(1)} %get-tuple-element.49), channel_id=1, source_target_pairs={{0,64},{32,96},{64,0},{96,32},{1,65},{33,97},{65,1},{97,33},{2,66}... | collective-permute-start | bytes 110600 | tf_op jit(solution)/shard_map/ppermute | solution.py:624
  89.9 0.6 collective-permute-start.11
  90.5 0.0 collective-permute-done.8.other_ref
  90.5 0.0 copy-done
  90.5 0.0 copy-done.2
  90.5 2.5 %slot_scores.1.rest_4_ = f32[512,256]{1,0:T(8,128)} custom-call(s32[5]{0:T(128)S(1)} %stack.23.place_ref, s32[4,512]{1,0:T(4,128)S(1)} %bitcast.16, f32[512,768]{1,0:T(8,128)S(1)} %copy-done, f32[768,128]{1,0:T(8,128)S(1)} %bitcast.14, f32[768,128]{1,0:T(8,128)S(1)} %collective-permute-done.8.other_ref), custom_call_target="tpu_custom_call" | custom-call | flops 603979776 | bytes 4000000 | tf_op jit(solution)/shard_map/slot_scores/pallas_call | solution.py:355
  93.1 0.0 collective-permute-done.9.rest_1_
  93.1 0.0 collective-permute-done.10.rest_2_
  93.1 0.8 collective-permute-done.11.rest_3_
  93.9 0.6 z_sums.1
  (1 shorter events, 0.0 us)
Async XLA Ops:
  0.6 4.0 %copy-start.6 = (s32[16]{0:T(128)S(1)}, s32[16]{0:T(128)}, u32[]{:S(2)}) copy-start(s32[16]{0:T(128)} %param.11) | copy-start | bytes 196
  0.6 4.1 %copy-start.4 = (f32[768]{0:T(1024)S(1)}, f32[768]{0:T(1024)}, u32[]{:S(2)}) copy-start(f32[768]{0:T(1024)} %param.13) | copy-start | bytes 9220
  0.7 18.2 %collective-permute-start.3 = (bf16[1024,768]{1,0:T(8,128)(2,1)}, bf16[1024,768]{1,0:T(8,128)(2,1)S(1)}, u32[]{:S(2)}, u32[]{:S(2)}) collective-permute-start(bf16[1024,768]{1,0:T(8,128)(2,1)} %bitcast.22), channel_id=1, source_target_pairs={{0,16},{16,0},{1,17},{17,1},{2,18},{18,2},{3,19},{19,3},{4,20},{20... | collective-permute-start | bytes 4718600 | tf_op jit(solution)/shard_map/ppermute | solution.py:620
  4.1 2.2 %collective-permute-start = (f32[1024,128]{1,0:T(8,128)S(1)}, f32[1024,128]{1,0:T(8,128)S(1)}, u32[]{:S(2)}, u32[]{:S(2)}) collective-permute-start(f32[1024,128]{1,0:T(8,128)S(1)} %get-tuple-element.29), channel_id=1, source_target_pairs={{0,16},{16,0},{1,17},{17,1},{2,18},{18,2},{3,19},{19,3},{4,20},{20... | collective-permute-start | bytes 1572872 | tf_op jit(solution)/shard_map/ppermute | solution.py:620
  4.7 1.5 %collective-permute-start.2 = (s32[16]{0:T(128)S(1)}, s32[16]{0:T(128)S(1)}, u32[]{:S(2)}, u32[]{:S(2)}) collective-permute-start(s32[16]{0:T(128)S(1)} %copy-done.6), channel_id=1, source_target_pairs={{0,16},{16,0},{1,17},{17,1},{2,18},{18,2},{3,19},{19,3},{4,20},{20... | collective-permute-start | bytes 200 | tf_op jit(solution)/shard_map/ppermute | solution.py:620
  7.1 26.7 %all-to-all-start = ((f32[64,16,128]{2,1,0:T(8,128)}), f32[64,16,128]{2,1,0:T(8,128)S(1)}, u32[]{:S(2)}, u32[]{:S(2)}) async-start(f32[64,16,128]{2,1,0:T(8,128)} %bitcast.7), calls=%async_computation | async-start | bytes 1048576 | tf_op jit(solution)/shard_map/all_to_all | solution.py:629
  18.8 1.1 %copy-start.5 = (bf16[1024,768]{1,0:T(8,128)(2,1)}, bf16[1024,768]{1,0:T(8,128)(2,1)S(1)}, u32[]{:S(2)}) copy-start(bf16[1024,768]{1,0:T(8,128)(2,1)S(1)} %collective-permute-done.3.other_ref) | copy-start | bytes 4718596
  20.0 13.8 %copy-start.3 = (s32[16,1]{0,1:T(1,128)S(1)}, s32[16,1]{0,1:T(1,128)}, u32[]{:S(2)}) copy-start(s32[16,1]{0,1:T(1,128)} %param.12) | copy-start | bytes 196
  20.0 15.5 %copy-start.1 = (f32[16,768]{1,0:T(8,128)S(1)}, f32[16,768]{1,0:T(8,128)}, u32[]{:S(2)}) copy-start(f32[16,768]{1,0:T(8,128)} %free_ref.1) | copy-start | bytes 147460
  33.6 1.9 %collective-permute-start.4 = (f32[32,768]{1,0:T(8,128)S(1)}, f32[32,768]{1,0:T(8,128)S(1)}, u32[]{:S(2)}, u32[]{:S(2)}) collective-permute-start(f32[32,768]{1,0:T(8,128)S(1)} %get-tuple-element.31.part_ref), channel_id=1, source_target_pairs={{0,16},{16,0},{1,17},{17,1},{2,18},{18,2},{3,19},{19,3},{4,20},{20... | collective-permute-start | bytes 294920 | tf_op jit(solution)/shard_map/ppermute | solution.py:620
  35.0 1.3 %collective-permute-start.1 = (f32[16,768]{1,0:T(8,128)S(1)}, f32[16,768]{1,0:T(8,128)S(1)}, u32[]{:S(2)}, u32[]{:S(2)}) collective-permute-start(f32[16,768]{1,0:T(8,128)S(1)} %get-tuple-element.30.free_own_ref), channel_id=1, source_target_pairs={{0,16},{16,0},{1,17},{17,1},{2,18},{18,2},{3,19},{19,3},{4,20},{20... | collective-permute-start | bytes 147464 | tf_op jit(solution)/shard_map/ppermute | solution.py:620
  37.0 15.1 %collective-permute-start.5 = (f32[448,128]{1,0:T(8,128)S(1)}, f32[448,128]{1,0:T(8,128)S(1)}, u32[]{:S(2)}, u32[]{:S(2)}) collective-permute-start(f32[448,128]{1,0:T(8,128)S(1)} %get-tuple-element.42), channel_id=1, source_target_pairs={{0,32},{32,64},{64,96},{96,0},{1,33},{33,65},{65,97},{97,1},{2,34}... | collective-permute-start | bytes 688136 | tf_op jit(solution)/shard_map/ppermute | solution.py:624
  38.5 13.6 %collective-permute-start.6 = (f32[448,128]{1,0:T(8,128)S(1)}, f32[448,128]{1,0:T(8,128)S(1)}, u32[]{:S(2)}, u32[]{:S(2)}) collective-permute-start(f32[448,128]{1,0:T(8,128)S(1)} %get-tuple-element.43), channel_id=1, source_target_pairs={{0,64},{32,96},{64,0},{96,32},{1,65},{33,97},{65,1},{97,33},{2,66}... | collective-permute-start | bytes 688136 | tf_op jit(solution)/shard_map/ppermute | solution.py:624
  41.4 10.8 %collective-permute-start.7 = (f32[448,128]{1,0:T(8,128)S(1)}, f32[448,128]{1,0:T(8,128)S(1)}, u32[]{:S(2)}, u32[]{:S(2)}) collective-permute-start(f32[448,128]{1,0:T(8,128)S(1)} %get-tuple-element.44), channel_id=1, source_target_pairs={{0,96},{32,0},{64,32},{96,64},{1,97},{33,1},{65,33},{97,65},{2,98}... | collective-permute-start | bytes 688136 | tf_op jit(solution)/shard_map/ppermute | solution.py:624
  83.9 6.6 %copy-start = (f32[512,768]{1,0:T(8,128)S(1)}, f32[512,768]{1,0:T(8,128)}, u32[]{:S(2)}) copy-start(f32[512,768]{1,0:T(8,128)} %queries_ref.3) | copy-start | bytes 4718596
  83.9 6.6 %copy-start.2 = (s32[512,4]{0,1:T(4,128)S(1)}, s32[512,4]{0,1:T(4,128)}, u32[]{:S(2)}) copy-start(s32[512,4]{0,1:T(4,128)} %param.18) | copy-start | bytes 24580
  85.6 4.9 %collective-permute-start.8 = (f32[768,128]{1,0:T(8,128)S(1)}, f32[768,128]{1,0:T(8,128)S(1)}, u32[]{:S(2)}, u32[]{:S(2)}) collective-permute-start(f32[768,128]{1,0:T(8,128)S(1)} %bitcast.13), channel_id=1, source_target_pairs={{0,16},{16,0},{1,17},{17,1},{2,18},{18,2},{3,19},{19,3},{4,20},{20... | collective-permute-start | bytes 1179656 | tf_op jit(solution)/shard_map/ppermute | solution.py:620
  85.6 7.4 %collective-permute-start.9 = (f32[72,128]{1,0:T(8,128)S(1)}, f32[72,128]{1,0:T(8,128)S(1)}, u32[]{:S(2)}, u32[]{:S(2)}) collective-permute-start(f32[72,128]{1,0:T(8,128)S(1)} %get-tuple-element.48), channel_id=1, source_target_pairs={{0,32},{32,64},{64,96},{96,0},{1,33},{33,65},{65,97},{97,1},{2,34}... | collective-permute-start | bytes 110600 | tf_op jit(solution)/shard_map/ppermute | solution.py:624
  86.6 6.4 %collective-permute-start.10 = (f32[72,128]{1,0:T(8,128)S(1)}, f32[72,128]{1,0:T(8,128)S(1)}, u32[]{:S(2)}, u32[]{:S(2)}) collective-permute-start(f32[72,128]{1,0:T(8,128)S(1)} %get-tuple-element.49), channel_id=1, source_target_pairs={{0,64},{32,96},{64,0},{96,32},{1,65},{33,97},{65,1},{97,33},{2,66}... | collective-permute-start | bytes 110600 | tf_op jit(solution)/shard_map/ppermute | solution.py:624
  89.9 4.0 %collective-permute-start.11 = (f32[72,128]{1,0:T(8,128)S(1)}, f32[72,128]{1,0:T(8,128)S(1)}, u32[]{:S(2)}, u32[]{:S(2)}) collective-permute-start(f32[72,128]{1,0:T(8,128)S(1)} %get-tuple-element.50), channel_id=1, source_target_pairs={{0,96},{32,0},{64,32},{96,64},{1,97},{33,1},{65,33},{97,65},{2,98}... | collective-permute-start | bytes 110600 | tf_op jit(solution)/shard_map/ppermute | solution.py:624

commit v3 on v2

--- a/solution.py
+++ b/solution.py
@@ -34,6 +34,7 @@
 PIECES = D // 128
 CHUNK = PIECES * ROWS
 SLOT_ROWS = CAP * PIECES
+CHIP_ROWS = N_CORE * SLOT_ROWS
 AT_W_OUT = N_Z * CHUNK
 AT_POWERS = AT_W_OUT + CHUNK
 AT_LABELS = AT_POWERS + 8
@@ -95,34 +96,33 @@
 NN, NT, TN = ((1,), (0,)), ((1,), (1,)), ((0,), (0,))
 
 
-def partial_kernel(place_ref, shortlist_ref, grad_ref, queries_ref, own_ref, other_ref):
+def partial_kernel(place_ref, shortlist_ref, grad_ref, queries_ref, out_ref):
     weighted = grad_ref[...] * is_kept(shortlist_ref, place_ref[1])
     size = 2 * CHIP_SLOTS
     target = iota((size, size), 1)
-    half = target // CHIP_SLOTS
+    core = target // CHIP_SLOTS
     rank = target // N_CHIPS % CAP
     z = target // N_LABEL % N_Z
     lab = target % N_LABEL
-    flip = jnp.where(half == 0, place_ref[0], 1 - place_ref[0])
-    source = ((z * N_CORE + flip) * N_LABEL + lab) * CAP + rank
+    source = ((z * N_CORE + core) * N_LABEL + lab) * CAP + rank
     order = (iota((size, size), 0) == source).astype(bf16)
     w_high, w_low = (dot(part, order, NN).astype(bf16) for part in split(weighted))
     q_high, q_low = split(queries_ref[...])
     total = dot(w_high, q_high, TN) + (dot(w_high, q_low, TN) + dot(w_low, q_high, TN))
-    for h, ref in enumerate((own_ref, other_ref)):
-        for r in range(CAP):
-            start = h * CHIP_SLOTS + r * N_CHIPS
-            for j in range(PIECES):
-                ref[pl.ds(PIECES * r + j, N_CHIPS, stride=16)] = total[start : start + N_CHIPS, j * 128 : (j + 1) * 128]
+    for k in range(N_CORE * CAP):
+        start = k * N_CHIPS
+        for j in range(PIECES):
+            out_ref[pl.ds(PIECES * k + j, N_CHIPS, stride=CHIP_ROWS)] = total[
+                start : start + N_CHIPS, j * 128 : (j + 1) * 128
+            ]
 
 
 def slot_partials(place, shortlist, grad_scores, queries):
-    shape = jax.ShapeDtypeStruct((N_CHIPS * 16, 128), f32)
     return pl.pallas_call(
         partial_kernel,
-        out_shape=(shape, shape),
+        out_shape=jax.ShapeDtypeStruct((N_CHIPS * CHIP_ROWS, 128), f32),
         in_specs=smem(1) + vmem(3),
-        out_specs=tuple(vmem(2)),
+        out_specs=pl.BlockSpec(memory_space=pltpu.VMEM),
         compiler_params=params(24),
         cost_estimate=cost(6 * QROWS * 256 * D, 4 * 10**6),
         name="slot_partials",
@@ -283,11 +283,11 @@
     return lax.rsqrt(jnp.sum(sums * sums, axis=-1, keepdims=True) + 1e-06)
 
 
-def each_label(owners_ref, counts, put):
+def each_label(owners_ref, counts, put, first=0):
     for o in range(N_LABEL):
         counts[o] = 0
     for i in range(TXT):
-        owner = owners_ref[i]
+        owner = owners_ref[first + i]
         rank = counts[owner]
         counts[owner] = rank + 1
         put(i, owner, jnp.minimum(rank, CAP - 1))
@@ -363,34 +363,40 @@
     )(place, shortlist, queries, own, other)
 
 
-def return_kernel(owners_ref, came_ref, out_ref, again_ref, counts):
-    def put(i, owner, rank):
-        value = came_ref[owner]
-        for z in range(1, N_Z):
-            value = value + came_ref[z * N_LABEL + owner]
-        value = jnp.where(rank == 0, value[:PIECES], value[PIECES : 2 * PIECES])
-        for j in range(PIECES):
-            out_ref[i : i + 1, j * 128 : (j + 1) * 128] = value[j : j + 1]
-            again_ref[i : i + 1, j * 128 : (j + 1) * 128] = value[j : j + 1]
-
-    each_label(owners_ref, counts, put)
-
-
-def returned(owners, came):
+def return_kernel(place_ref, owners_ref, came_ref, out_ref, counts):
+    for h in range(N_CORE):
+        core = place_ref[0] if h == 0 else 1 - place_ref[0]
+
+        def put(i, owner, rank, h=h, core=core):
+            value = came_ref[owner]
+            for z in range(1, N_Z):
+                value = value + came_ref[z * N_LABEL + owner]
+            value = jnp.where(core == 0, value[:SLOT_ROWS], value[SLOT_ROWS:])
+            value = jnp.where(rank == 0, value[:PIECES], value[PIECES:])
+            row = h * TXT + i
+            for j in range(PIECES):
+                out_ref[row : row + 1, j * 128 : (j + 1) * 128] = value[j : j + 1]
+
+        each_label(owners_ref, counts, put, h * TXT)
+
+
+def returned(place, owners, came):
     return pl.pallas_call(
         return_kernel,
-        out_shape=(jax.ShapeDtypeStruct((TXT, D), f32),) * 2,
-        in_specs=smem(1) + vmem(1),
-        out_specs=tuple(vmem(2)),
+        out_shape=jax.ShapeDtypeStruct((2 * TXT, D), f32),
+        in_specs=smem(2) + vmem(1),
+        out_specs=pl.BlockSpec(memory_space=pltpu.VMEM),
         scratch_shapes=[pltpu.SMEM((N_LABEL,), jnp.int32)],
         compiler_params=params(8),
         cost_estimate=cost(10**5, 5 * 10**5),
         name="returned_gradients",
-    )(owners, came)
-
-
-def pull_kernel(place_ref, free_own_ref, free_other_ref, sums_ref, pooled_ref, labels_ref, pulled_ref, *outs):
-    free = jnp.concatenate([free_own_ref[...], free_other_ref[...]], axis=0)
+    )(place, owners, came)
+
+
+def pull_kernel(place_ref, free_ref, came_ref, sums_ref, pooled_ref, labels_ref, pulled_ref, free_grad_ref, *outs):
+    own = free_ref[:TXT] + came_ref[TXT:]
+    free_grad_ref[...] = own
+    free = jnp.concatenate([own, free_ref[TXT:] + came_ref[:TXT]], axis=0)
     sums = sums_ref[...]
     unit = unit_rows(sums)
     along = jnp.sum(sums * free, axis=-1, keepdims=True)
@@ -404,17 +410,17 @@
         outs[f][FACTOR_ROWS:] = labels_ref[...]
 
 
-def pull(place, free_own, free_other, sums, pooled, label_rows):
+def pull(place, free, came, sums, pooled, label_rows):
     return pl.pallas_call(
         pull_kernel,
-        out_shape=(jax.ShapeDtypeStruct((2 * TXT, HALF), f32),)
+        out_shape=(jax.ShapeDtypeStruct((2 * TXT, D), f32), jax.ShapeDtypeStruct((TXT, D), f32))
         + (jax.ShapeDtypeStruct((MOVED_ROWS, 128), f32),) * N_Z,
         in_specs=smem(1) + vmem(5),
-        out_specs=tuple(vmem(1 + N_Z)),
+        out_specs=tuple(vmem(2 + N_Z)),
         compiler_params=params(12),
         cost_estimate=cost(6 * 32 * HALF * D, 3 * 10**6),
         name="pull_back",
-    )(place, free_own, free_other, sums, pooled, label_rows)
+    )(place, free, came, sums, pooled, label_rows)
 
 
 def w_out_kernel(pulled_ref, high_ref, low_ref, back_ref):
@@ -634,21 +640,23 @@
     place = jnp.stack([core, x * N_Y + y, x, y, z]).astype(jnp.int32)
     own = texts.reshape(TXT * LMAX, D)
     other = swap(own)
-    both_lengths = jnp.concatenate([lengths, swap(lengths)])
-    owner_ids = owners[:, 0]
+    ints = jnp.stack([lengths, owners[:, 0]])
+    ints_other = swap(ints)
+    both_lengths = jnp.concatenate([ints[0], ints_other[0]])
+    owner_ids = jnp.concatenate([ints[1], ints_other[1]])
     names = shortlist.T
     gain_row = gain.reshape(1, D)
     w_in_blocks = w_in.reshape(N_Z, N_CORE, BLOCK, D)
     w_out_blocks = w_out.reshape(N_Z, N_CORE, BLOCK, D)
 
-    kept, sent = slot_partials(place, names, grad_scores, queries)
-    slots = exchange((kept + swap(sent)).reshape(N_CHIPS, 16, 128), ("z", "x", "y"))
+    slots = slot_partials(place, names, grad_scores, queries).reshape(N_CHIPS, CHIP_ROWS, 128)
+    slots = exchange(slots, ("z", "x", "y"))
 
     slope, pooled, part, high, low = forward(place, both_lengths, gain_row, own, other, w_in_blocks, w_out_blocks)
     sums, label_rows = labels(owner_ids, part, swap(part), free_vectors)
 
-    free_grad, free_own = returned(owner_ids, slots)
-    pulled, *factors = pull(place, free_own, swap(free_own), sums, pooled, label_rows)
+    free = returned(place, owner_ids, slots)
+    pulled, free_grad, *factors = pull(place, free, swap(free), sums, pooled, label_rows)
     back = through_w_out(pulled, high, low)
     factors = shift(factors, "z")
     grad, largest = backward(back, gain_row, own, other, slope)

time: 94.8 us -> 94 us (level)
  starting transfers between devices: 23.6 us -> 22.2 us
    ppermute x6 -> x5, waiting for transfers between devices: 1.62 us -> 0.59 us  [swap(): return lax.ppermute(value, 'core', ((0, 1), (1, 0)))]
  transfers between devices with their start and end apart: 13 -> 12, of which waited for: 3 -> 4; matrix products, arithmetic and copies ran while one was open for 1% -> 1% of each run, Pallas kernels for 32% -> 33%
where the time goes in v3:
time: 94 us; the launch traced here: 93.7 us
  Pallas kernels  35.5 us (38%)
  blocking collectives  30.2 us (32%)
  starting transfers between devices  22.2 us (24%)
  waiting for transfers between devices  2.34 us (2%)
  other arithmetic  1.39 us (1%)
  local copies, waits for them, and re-layouts  1.27 us (1%)
    all_to_all x1, blocking collectives, exchange(): return lax.all_to_all(value, axes, split_axis=0, concat_axis=0, tiled=True)  30.2 us
    pallas_call x1, Pallas kernels, forward(): pl.pallas_call(forward_kernel, out_shape=(pltpu.HBM((tokens, HALF), f32),...  13.6 us
    all_to_all x1, starting transfers between devices, exchange(): return lax.all_to_all(value, axes, split_axis=0, concat_axis=0, tiled=True)  11.7 us
    ppermute x6, starting transfers between devices, shift(): lax.ppermute(blocks[k], axis, [(i, (i + k) % 4) for i in range(4)])  9.78 us
    pallas_call x1, Pallas kernels, backward(): pl.pallas_call(backward_kernel, out_shape=(shape((HALF, D), f32), shape((...  8.14 us
    pallas_call x1, Pallas kernels, slot_partials(): pl.pallas_call(partial_kernel, out_shape=jax.ShapeDtypeStruct((N_CHIPS *...  4.17 us
    pallas_call x1, Pallas kernels, slot_scores(): pl.pallas_call(scores_kernel, out_shape=jax.ShapeDtypeStruct((QROWS, 2 *...  2.51 us
  transfers between devices with their start and end apart: 12, of which 4 were waited for; matrix products, arithmetic and copies ran while one was open for 1% of the time, Pallas kernels for 33%

profile of v3, /device:TPU:0, one launch (start us, length us, event | category | flops | bytes accessed | tf_op | source)
XLA Modules:
  0.0 93.7 jit_solution(4244700685052280853)
XLA Ops:
  0.6 0.1 collective-permute-start.2
  0.7 0.7 pad_add_fusion
  1.4 0.5 collective-permute-start
  1.9 0.1 stack.29.place_ref
  2.0 0.0 copy-start.3
  2.0 0.0 copy-start.4
  2.0 4.2 %slot_partials.1 = f32[1536,128]{1,0:T(8,128)} custom-call(s32[5]{0:T(128)S(1)} %stack.29.place_ref, s32[4,512]{1,0:T(4,128)} %bitcast.21, f32[512,256]{1,0:T(8,128)} %grad_ref.1, f32[512,768]{1,0:T(8,128)} %queries_ref.3), custom_call_target="tpu_custom_call" | custom-call | flops 603979776 | bytes 4000000 | tf_op jit(solution)/shard_map/slot_partials/pallas_call | solution.py:121
  6.2 11.7 %all-to-all-start = ((f32[64,24,128]{2,1,0:T(8,128)}), f32[64,24,128]{2,1,0:T(8,128)S(1)}, u32[]{:S(2)}, u32[]{:S(2)}) async-start(f32[64,24,128]{2,1,0:T(8,128)} %bitcast.10), calls=%async_computation | async-start | bytes 1572864 | tf_op jit(solution)/shard_map/all_to_all | solution.py:635
  17.8 0.0 copy-done.3
  17.9 0.0 collective-permute-done
  17.9 0.0 copy-done.4
  17.9 0.1 pad_add_fusion.2.lengths_ref
  18.0 0.0 collective-permute-done.2.other_ref
  18.0 0.0 copy-start.6
  18.0 1.2 %copy-done.6 = bf16[1024,768]{1,0:T(8,128)(2,1)} copy-done((bf16[1024,768]{1,0:T(8,128)(2,1)}, bf16[1024,768]{1,0:T(8,128)(2,1)S(1)}, u32[]{:S(2)}) %copy-start.6) | copy-done | bytes 1572888
  19.1 0.0 copy-start.5
  19.1 0.0 copy-start.1
  19.1 13.6 %encoder_forward.1 = (f32[2048,768]{1,0:T(8,128)}, f32[4,32,256]{2,1,0:T(8,128)S(1)}, f32[32,768]{1,0:T(8,128)S(1)}, bf16[4,192,768]{2,1,0:T(8,128)(2,1)S(1)}, bf16[4,192,768]{2,1,0:T(8,128)(2,1)S(1)}) custom-call(s32[5]{0:T(128)S(1)} %stack.29.place_ref, s32[32]{0:T(128)S(1)} %pad_add_fusion.2.lengths_ref, f32[1,768]{1,0:T(1,128)S(1)} %reshape.29.gain_ref, ...), custom_call_target="tpu_custom_call" | custom-call | flops 12079595520 | bytes 8000000 | tf_op jit(solution)/shard_map/encoder_forward/pallas_call | solution.py:249
  32.8 0.1 collective-permute-start.3
  32.9 0.0 copy-done.5
  32.9 0.1 pad_add_fusion.1.owners_ref
  33.0 0.9 all-to-all-done.came_ref
  33.8 0.7 returned_gradients.1.free_ref
  34.6 0.1 collective-permute-start.1
  34.7 0.0 collective-permute-done.3.came_ref
  34.7 0.0 copy-done.1
  34.7 0.7 label_vectors.1
  35.4 0.6 collective-permute-done.1.came_ref
  36.0 1.2 %pull_back.1 = (f32[32,768]{1,0:T(8,128)S(1)}, f32[16,768]{1,0:T(8,128)}, f32[448,128]{1,0:T(8,128)S(1)}, f32[448,128]{1,0:T(8,128)S(1)}, f32[448,128]{1,0:T(8,128)S(1)}, /*index=5*/f32[448,128]{1,0:T(8,128)S(1)}) custom-call(s32[5]{0:T(128)S(1)} %stack.29.place_ref, f32[32,768]{1,0:T(8,128)S(1)} %returned_gradients.1.free_ref, ...), custom_call_target="tpu_custom_call" | custom-call | flops 113246208 | bytes 3000000 | tf_op jit(solution)/shard_map/pull_back/pallas_call | solution.py:414
  37.2 0.7 collective-permute-start.4
  37.8 2.9 %collective-permute-start.5 = (f32[448,128]{1,0:T(8,128)S(1)}, f32[448,128]{1,0:T(8,128)S(1)}, u32[]{:S(2)}, u32[]{:S(2)}) collective-permute-start(f32[448,128]{1,0:T(8,128)S(1)} %get-tuple-element.37), channel_id=1, source_target_pairs={{0,64},{32,96},{64,0},{96,32},{1,65},{33,97},{65,1},{97,33},{2,66}... | collective-permute-start | bytes 688136 | tf_op jit(solution)/shard_map/ppermute | solution.py:630
  40.7 1.4 %collective-permute-start.6 = (f32[448,128]{1,0:T(8,128)S(1)}, f32[448,128]{1,0:T(8,128)S(1)}, u32[]{:S(2)}, u32[]{:S(2)}) collective-permute-start(f32[448,128]{1,0:T(8,128)S(1)} %get-tuple-element.38), channel_id=1, source_target_pairs={{0,96},{32,0},{64,32},{96,64},{1,97},{33,1},{65,33},{97,65},{2,98}... | collective-permute-start | bytes 688136 | tf_op jit(solution)/shard_map/ppermute | solution.py:630
  42.1 1.2 %back_through_w_out.1.back_ref = f32[32,768]{1,0:T(8,128)S(1)} custom-call(f32[32,768]{1,0:T(8,128)S(1)} %get-tuple-element.29.pulled_ref, bf16[4,192,768]{2,1,0:T(8,128)(2,1)S(1)} %get-tuple-element.30.high_ref, bf16[4,192,768]{2,1,0:T(8,128)(2,1)S(1)} %get-tuple-element.31.low_ref), custom_call_target="tpu_custom_call" | custom-call | flops 113246208 | bytes 3000000 | tf_op jit(solution)/shard_map/back_through_w_out/pallas_call | solution.py:438
  43.3 8.1 %encoder_backward.1 = (f32[768,768]{1,0:T(8,128)S(1)}, f32[3,768]{1,0:T(4,128)S(1)}) custom-call(f32[32,768]{1,0:T(8,128)S(1)} %back_through_w_out.1.back_ref, f32[1,768]{1,0:T(1,128)S(1)} %reshape.29.gain_ref, bf16[1024,768]{1,0:T(8,128)(2,1)} %bitcast.31, bf16[1024,768]{1,0:T(8,128)(2,1)} %copy-done.6, f32[2048,768]{1,0:T(8,128)} %get-tuple-element.32.slope_ref), custom_call_target="tpu_custom_call" | custom-call | flops 6039797760 | bytes 4000000 | tf_op jit(solution)/shard_map/encoder_backward/pallas_call | solution.py:495
  51.4 0.0 collective-permute-done.4.rest_1_
  51.4 0.0 collective-permute-done.5.rest_2_
  51.4 0.1 collective-permute-done.6.rest_3_
  51.6 0.9 finish_gradients.1
  52.5 0.2 convert_element_type.9
  52.7 30.2 %all_to_all.10 = f16[16,416,128]{2,1,0:T(8,128)(2,1)S(1)} all-to-all(f16[16,416,128]{2,1,0:T(8,128)(2,1)S(1)} %bitcast.23), channel_id=1, replica_groups=mesh['z'=4,'core'=2,'x'=4,'y'=4] {'x','y'}, dimensions={0} | all-to-all | bytes 3407872 | tf_op jit(solution)/shard_map/all_to_all | solution.py:635
  82.9 0.3 convert_element_type.11.came_ref
  83.2 0.0 copy-start
  83.3 0.0 copy-start.2
  83.3 1.7 %plane_sums.1 = (f32[12,768]{1,0:T(8,128)}, f32[4,192,128]{2,1,0:T(8,128)S(1)}, f32[72,128]{1,0:T(8,128)S(1)}, f32[72,128]{1,0:T(8,128)S(1)}, f32[72,128]{1,0:T(8,128)S(1)}, /*index=5*/f32[72,128]{1,0:T(8,128)S(1)}) custom-call(s32[5]{0:T(128)S(1)} %stack.29.place_ref, f32[16,416,128]{2,1,0:T(8,128)S(1)} %convert_element_type.11.came_ref), custom_call_target="tpu_custom_call" | custom-call | flops 10000000 | bytes 4000000 | tf_op jit(solution)/shard_map/plane_sums/pallas_call | solution.py:593
  84.9 0.0 collective-permute-start.7
  85.0 0.8 collective-permute-start.8
  85.8 3.4 %collective-permute-start.9 = (f32[72,128]{1,0:T(8,128)S(1)}, f32[72,128]{1,0:T(8,128)S(1)}, u32[]{:S(2)}, u32[]{:S(2)}) collective-permute-start(f32[72,128]{1,0:T(8,128)S(1)} %get-tuple-element.43), channel_id=1, source_target_pairs={{0,64},{32,96},{64,0},{96,32},{1,65},{33,97},{65,1},{97,33},{2,66}... | collective-permute-start | bytes 110600 | tf_op jit(solution)/shard_map/ppermute | solution.py:630
  89.1 0.7 collective-permute-start.10
  89.8 0.0 collective-permute-done.7.other_ref
  89.8 0.0 copy-done
  89.8 0.0 copy-done.2
  89.8 2.5 %slot_scores.1.rest_4_ = f32[512,256]{1,0:T(8,128)} custom-call(s32[5]{0:T(128)S(1)} %stack.29.place_ref, s32[4,512]{1,0:T(4,128)S(1)} %bitcast.22, f32[512,768]{1,0:T(8,128)S(1)} %copy-done, f32[768,128]{1,0:T(8,128)S(1)} %bitcast.20, f32[768,128]{1,0:T(8,128)S(1)} %collective-permute-done.7.other_ref), custom_call_target="tpu_custom_call" | custom-call | flops 603979776 | bytes 4000000 | tf_op jit(solution)/shard_map/slot_scores/pallas_call | solution.py:355
  92.4 0.0 collective-permute-done.8.rest_1_
  92.4 0.0 collective-permute-done.9.rest_2_
  92.4 0.7 collective-permute-done.10.rest_3_
  93.1 0.6 z_sums.1
  (2 shorter events, 0.0 us)
Async XLA Ops:
  0.6 17.3 %collective-permute-start.2 = (bf16[1024,768]{1,0:T(8,128)(2,1)}, bf16[1024,768]{1,0:T(8,128)(2,1)S(1)}, u32[]{:S(2)}, u32[]{:S(2)}) collective-permute-start(bf16[1024,768]{1,0:T(8,128)(2,1)} %bitcast.29), channel_id=1, source_target_pairs={{0,16},{16,0},{1,17},{17,1},{2,18},{18,2},{3,19},{19,3},{4,20},{20... | collective-permute-start | bytes 4718600 | tf_op jit(solution)/shard_map/ppermute | solution.py:626
  1.4 16.5 %collective-permute-start = (s32[2,16]{1,0:T(2,128)S(1)}, s32[2,16]{1,0:T(2,128)S(1)}, u32[]{:S(2)}, u32[]{:S(2)}) collective-permute-start(s32[2,16]{1,0:T(2,128)S(1)} %pad_add_fusion), channel_id=1, source_target_pairs={{0,16},{16,0},{1,17},{17,1},{2,18},{18,2},{3,19},{19,3},{4,20},{20... | collective-permute-start | bytes 392 | tf_op jit(solution)/shard_map/ppermute | solution.py:626
  2.0 15.9 %copy-start.3 = (f32[768]{0:T(1024)S(1)}, f32[768]{0:T(1024)}, u32[]{:S(2)}) copy-start(f32[768]{0:T(1024)} %param.13) | copy-start | bytes 9220
  2.0 15.9 %copy-start.4 = (s32[16]{0:T(128)S(1)}, s32[16]{0:T(128)}, u32[]{:S(2)}) copy-start(s32[16]{0:T(128)} %param.11) | copy-start | bytes 196
  6.2 27.7 %all-to-all-start = ((f32[64,24,128]{2,1,0:T(8,128)}), f32[64,24,128]{2,1,0:T(8,128)S(1)}, u32[]{:S(2)}, u32[]{:S(2)}) async-start(f32[64,24,128]{2,1,0:T(8,128)} %bitcast.10), calls=%async_computation | async-start | bytes 1572864 | tf_op jit(solution)/shard_map/all_to_all | solution.py:635
  18.0 1.2 %copy-start.6 = (bf16[1024,768]{1,0:T(8,128)(2,1)}, bf16[1024,768]{1,0:T(8,128)(2,1)S(1)}, u32[]{:S(2)}) copy-start(bf16[1024,768]{1,0:T(8,128)(2,1)S(1)} %collective-permute-done.2.other_ref) | copy-start | bytes 4718596
  19.1 13.7 %copy-start.5 = (s32[16,1]{0,1:T(1,128)S(1)}, s32[16,1]{0,1:T(1,128)}, u32[]{:S(2)}) copy-start(s32[16,1]{0,1:T(1,128)} %param.12) | copy-start | bytes 196
  19.1 15.5 %copy-start.1 = (f32[16,768]{1,0:T(8,128)S(1)}, f32[16,768]{1,0:T(8,128)}, u32[]{:S(2)}) copy-start(f32[16,768]{1,0:T(8,128)} %free_ref.1) | copy-start | bytes 147460
  32.8 1.9 %collective-permute-start.3 = (f32[32,768]{1,0:T(8,128)S(1)}, f32[32,768]{1,0:T(8,128)S(1)}, u32[]{:S(2)}, u32[]{:S(2)}) collective-permute-start(f32[32,768]{1,0:T(8,128)S(1)} %get-tuple-element.25.part_ref), channel_id=1, source_target_pairs={{0,16},{16,0},{1,17},{17,1},{2,18},{18,2},{3,19},{19,3},{4,20},{20... | collective-permute-start | bytes 294920 | tf_op jit(solution)/shard_map/ppermute | solution.py:626
  34.6 1.4 %collective-permute-start.1 = (f32[32,768]{1,0:T(8,128)S(1)}, f32[32,768]{1,0:T(8,128)S(1)}, u32[]{:S(2)}, u32[]{:S(2)}) collective-permute-start(f32[32,768]{1,0:T(8,128)S(1)} %returned_gradients.1.free_ref), channel_id=1, source_target_pairs={{0,16},{16,0},{1,17},{17,1},{2,18},{18,2},{3,19},{19,3},{4,20},{20... | collective-permute-start | bytes 294920 | tf_op jit(solution)/shard_map/ppermute | solution.py:626
  37.2 14.3 %collective-permute-start.4 = (f32[448,128]{1,0:T(8,128)S(1)}, f32[448,128]{1,0:T(8,128)S(1)}, u32[]{:S(2)}, u32[]{:S(2)}) collective-permute-start(f32[448,128]{1,0:T(8,128)S(1)} %get-tuple-element.36), channel_id=1, source_target_pairs={{0,32},{32,64},{64,96},{96,0},{1,33},{33,65},{65,97},{97,1},{2,34}... | collective-permute-start | bytes 688136 | tf_op jit(solution)/shard_map/ppermute | solution.py:630
  37.8 13.6 %collective-permute-start.5 = (f32[448,128]{1,0:T(8,128)S(1)}, f32[448,128]{1,0:T(8,128)S(1)}, u32[]{:S(2)}, u32[]{:S(2)}) collective-permute-start(f32[448,128]{1,0:T(8,128)S(1)} %get-tuple-element.37), channel_id=1, source_target_pairs={{0,64},{32,96},{64,0},{96,32},{1,65},{33,97},{65,1},{97,33},{2,66}... | collective-permute-start | bytes 688136 | tf_op jit(solution)/shard_map/ppermute | solution.py:630
  40.7 10.9 %collective-permute-start.6 = (f32[448,128]{1,0:T(8,128)S(1)}, f32[448,128]{1,0:T(8,128)S(1)}, u32[]{:S(2)}, u32[]{:S(2)}) collective-permute-start(f32[448,128]{1,0:T(8,128)S(1)} %get-tuple-element.38), channel_id=1, source_target_pairs={{0,96},{32,0},{64,32},{96,64},{1,97},{33,1},{65,33},{97,65},{2,98}... | collective-permute-start | bytes 688136 | tf_op jit(solution)/shard_map/ppermute | solution.py:630
  83.2 6.6 %copy-start = (f32[512,768]{1,0:T(8,128)S(1)}, f32[512,768]{1,0:T(8,128)}, u32[]{:S(2)}) copy-start(f32[512,768]{1,0:T(8,128)} %queries_ref.3) | copy-start | bytes 4718596
  83.3 6.6 %copy-start.2 = (s32[512,4]{0,1:T(4,128)S(1)}, s32[512,4]{0,1:T(4,128)}, u32[]{:S(2)}) copy-start(s32[512,4]{0,1:T(4,128)} %param.18) | copy-start | bytes 24580
  84.9 4.9 %collective-permute-start.7 = (f32[768,128]{1,0:T(8,128)S(1)}, f32[768,128]{1,0:T(8,128)S(1)}, u32[]{:S(2)}, u32[]{:S(2)}) collective-permute-start(f32[768,128]{1,0:T(8,128)S(1)} %bitcast.19), channel_id=1, source_target_pairs={{0,16},{16,0},{1,17},{17,1},{2,18},{18,2},{3,19},{19,3},{4,20},{20... | collective-permute-start | bytes 1179656 | tf_op jit(solution)/shard_map/ppermute | solution.py:626
  85.0 7.4 %collective-permute-start.8 = (f32[72,128]{1,0:T(8,128)S(1)}, f32[72,128]{1,0:T(8,128)S(1)}, u32[]{:S(2)}, u32[]{:S(2)}) collective-permute-start(f32[72,128]{1,0:T(8,128)S(1)} %get-tuple-element.42), channel_id=1, source_target_pairs={{0,32},{32,64},{64,96},{96,0},{1,33},{33,65},{65,97},{97,1},{2,34}... | collective-permute-start | bytes 110600 | tf_op jit(solution)/shard_map/ppermute | solution.py:630
  85.8 6.6 %collective-permute-start.9 = (f32[72,128]{1,0:T(8,128)S(1)}, f32[72,128]{1,0:T(8,128)S(1)}, u32[]{:S(2)}, u32[]{:S(2)}) collective-permute-start(f32[72,128]{1,0:T(8,128)S(1)} %get-tuple-element.43), channel_id=1, source_target_pairs={{0,64},{32,96},{64,0},{96,32},{1,65},{33,97},{65,1},{97,33},{2,66}... | collective-permute-start | bytes 110600 | tf_op jit(solution)/shard_map/ppermute | solution.py:630
  89.1 4.0 %collective-permute-start.10 = (f32[72,128]{1,0:T(8,128)S(1)}, f32[72,128]{1,0:T(8,128)S(1)}, u32[]{:S(2)}, u32[]{:S(2)}) collective-permute-start(f32[72,128]{1,0:T(8,128)S(1)} %get-tuple-element.44), channel_id=1, source_target_pairs={{0,96},{32,0},{64,32},{96,64},{1,97},{33,1},{65,33},{97,65},{2,98}... | collective-permute-start | bytes 110600 | tf_op jit(solution)/shard_map/ppermute | solution.py:630

commit v4 on v3

--- a/solution.py
+++ b/solution.py
@@ -393,9 +393,9 @@
     )(place, owners, came)
 
 
-def pull_kernel(place_ref, free_ref, came_ref, sums_ref, pooled_ref, labels_ref, pulled_ref, free_grad_ref, *outs):
+def pull_kernel(place_ref, free_ref, came_ref, sums_ref, pooled_ref, labels_ref, pulled_ref, joined_ref, *outs):
     own = free_ref[:TXT] + came_ref[TXT:]
-    free_grad_ref[...] = own
+    joined_ref[...] = own
     free = jnp.concatenate([own, free_ref[TXT:] + came_ref[:TXT]], axis=0)
     sums = sums_ref[...]
     unit = unit_rows(sums)
@@ -423,7 +423,8 @@
     )(place, free, came, sums, pooled, label_rows)
 
 
-def w_out_kernel(pulled_ref, high_ref, low_ref, back_ref):
+def w_out_kernel(pulled_ref, joined_ref, high_ref, low_ref, back_ref, free_grad_ref):
+    free_grad_ref[...] = joined_ref[...]
     p_high, p_low = split(pulled_ref[...])
     back_ref[...] = jnp.concatenate(
         [
@@ -434,16 +435,16 @@
     )
 
 
-def through_w_out(pulled, high, low):
+def through_w_out(pulled, joined, high, low):
     return pl.pallas_call(
         w_out_kernel,
-        out_shape=jax.ShapeDtypeStruct((2 * TXT, HALF), f32),
-        in_specs=vmem(3),
-        out_specs=pl.BlockSpec(memory_space=pltpu.VMEM),
+        out_shape=(jax.ShapeDtypeStruct((2 * TXT, HALF), f32), jax.ShapeDtypeStruct((TXT, D), f32)),
+        in_specs=vmem(4),
+        out_specs=tuple(vmem(2)),
         compiler_params=params(12),
         cost_estimate=cost(6 * 32 * HALF * D, 3 * 10**6),
         name="back_through_w_out",
-    )(pulled, high, low)
+    )(pulled, joined, high, low)
 
 
 def backward_kernel(back_ref, gain_ref, own_ref, other_ref, slope_ref, grad, largest, x_buf, slope_buf, sem):
@@ -656,8 +657,8 @@
     sums, label_rows = labels(owner_ids, part, swap(part), free_vectors)
 
     free = returned(place, owner_ids, slots)
-    pulled, free_grad, *factors = pull(place, free, swap(free), sums, pooled, label_rows)
-    back = through_w_out(pulled, high, low)
+    pulled, joined, *factors = pull(place, free, swap(free), sums, pooled, label_rows)
+    back, free_grad = through_w_out(pulled, joined, high, low)
     factors = shift(factors, "z")
     grad, largest = backward(back, gain_row, own, other, slope)
     sent_rows = finish(grad, largest, factors).reshape(N_LABEL, SENT_ROWS, 128)

time: 94 us -> 93.6 us (level)
  transfers between devices with their start and end apart: 12 -> 12, of which waited for: 4 -> 3; matrix products, arithmetic and copies ran while one was open for 1% -> 1% of each run, Pallas kernels for 33% -> 34%
where the time goes in v4:
time: 93.6 us; the launch traced here: 93.3 us
  Pallas kernels  35.3 us (38%)
  blocking collectives  30.3 us (32%)
  starting transfers between devices  22 us (24%)
  waiting for transfers between devices  2.29 us (2%)
  other arithmetic  1.39 us (1%)
  local copies, waits for them, and re-layouts  1.27 us (1%)
    all_to_all x1, blocking collectives, exchange(): return lax.all_to_all(value, axes, split_axis=0, concat_axis=0, tiled=True)  30.3 us
    pallas_call x1, Pallas kernels, forward(): pl.pallas_call(forward_kernel, out_shape=(pltpu.HBM((tokens, HALF), f32),...  13.6 us
    all_to_all x1, starting transfers between devices, exchange(): return lax.all_to_all(value, axes, split_axis=0, concat_axis=0, tiled=True)  11.7 us
    ppermute x6, starting transfers between devices, shift(): lax.ppermute(blocks[k], axis, [(i, (i + k) % 4) for i in range(4)])  9.53 us
    pallas_call x1, Pallas kernels, backward(): pl.pallas_call(backward_kernel, out_shape=(shape((HALF, D), f32), shape((...  8.11 us
    pallas_call x1, Pallas kernels, slot_partials(): pl.pallas_call(partial_kernel, out_shape=jax.ShapeDtypeStruct((N_CHIPS *...  4.17 us
    pallas_call x1, Pallas kernels, slot_scores(): pl.pallas_call(scores_kernel, out_shape=jax.ShapeDtypeStruct((QROWS, 2 *...  2.51 us
  transfers between devices with their start and end apart: 12, of which 3 were waited for; matrix products, arithmetic and copies ran while one was open for 1% of the time, Pallas kernels for 34%

profile of v4, /device:TPU:0, one launch (start us, length us, event | category | flops | bytes accessed | tf_op | source)
XLA Modules:
  0.0 93.3 jit_solution(13778938647331026099)
XLA Ops:
  0.6 0.1 collective-permute-start.2
  0.7 0.7 pad_add_fusion
  1.4 0.5 collective-permute-start
  1.9 0.1 stack.29.place_ref
  2.0 0.0 copy-start.3
  2.0 0.0 copy-start.4
  2.0 4.2 %slot_partials.1 = f32[1536,128]{1,0:T(8,128)} custom-call(s32[5]{0:T(128)S(1)} %stack.29.place_ref, s32[4,512]{1,0:T(4,128)} %bitcast.21, f32[512,256]{1,0:T(8,128)} %grad_ref.1, f32[512,768]{1,0:T(8,128)} %queries_ref.3), custom_call_target="tpu_custom_call" | custom-call | flops 603979776 | bytes 4000000 | tf_op jit(solution)/shard_map/slot_partials/pallas_call | solution.py:121
  6.2 11.7 %all-to-all-start = ((f32[64,24,128]{2,1,0:T(8,128)}), f32[64,24,128]{2,1,0:T(8,128)S(1)}, u32[]{:S(2)}, u32[]{:S(2)}) async-start(f32[64,24,128]{2,1,0:T(8,128)} %bitcast.10), calls=%async_computation | async-start | bytes 1572864 | tf_op jit(solution)/shard_map/all_to_all | solution.py:636
  17.8 0.0 copy-done.3
  17.9 0.0 collective-permute-done
  17.9 0.0 copy-done.4
  17.9 0.1 pad_add_fusion.2.lengths_ref
  18.0 0.0 collective-permute-done.2.other_ref
  18.0 0.0 copy-start.6
  18.0 1.1 %copy-done.6 = bf16[1024,768]{1,0:T(8,128)(2,1)} copy-done((bf16[1024,768]{1,0:T(8,128)(2,1)}, bf16[1024,768]{1,0:T(8,128)(2,1)S(1)}, u32[]{:S(2)}) %copy-start.6) | copy-done | bytes 1572888
  19.1 0.0 copy-start.5
  19.1 0.0 copy-start.1
  19.1 13.6 %encoder_forward.1 = (f32[2048,768]{1,0:T(8,128)}, f32[4,32,256]{2,1,0:T(8,128)S(1)}, f32[32,768]{1,0:T(8,128)S(1)}, bf16[4,192,768]{2,1,0:T(8,128)(2,1)S(1)}, bf16[4,192,768]{2,1,0:T(8,128)(2,1)S(1)}) custom-call(s32[5]{0:T(128)S(1)} %stack.29.place_ref, s32[32]{0:T(128)S(1)} %pad_add_fusion.2.lengths_ref, f32[1,768]{1,0:T(1,128)S(1)} %reshape.29.gain_ref, ...), custom_call_target="tpu_custom_call" | custom-call | flops 12079595520 | bytes 8000000 | tf_op jit(solution)/shard_map/encoder_forward/pallas_call | solution.py:249
  32.8 0.1 collective-permute-start.3
  32.9 0.0 copy-done.5
  32.9 0.1 pad_add_fusion.1.owners_ref
  33.0 0.9 all-to-all-done.came_ref
  33.8 0.7 returned_gradients.1.free_ref
  34.6 0.1 collective-permute-start.1
  34.7 0.0 collective-permute-done.3.came_ref
  34.7 0.0 copy-done.1
  34.7 0.7 label_vectors.1
  35.4 0.6 collective-permute-done.1.came_ref
  35.9 0.7 pull_back.1
  36.6 0.7 collective-permute-start.4
  37.4 2.9 %collective-permute-start.5 = (f32[448,128]{1,0:T(8,128)S(1)}, f32[448,128]{1,0:T(8,128)S(1)}, u32[]{:S(2)}, u32[]{:S(2)}) collective-permute-start(f32[448,128]{1,0:T(8,128)S(1)} %get-tuple-element.41), channel_id=1, source_target_pairs={{0,64},{32,96},{64,0},{96,32},{1,65},{33,97},{65,1},{97,33},{2,66}... | collective-permute-start | bytes 688136 | tf_op jit(solution)/shard_map/ppermute | solution.py:631
  40.2 1.4 %collective-permute-start.6 = (f32[448,128]{1,0:T(8,128)S(1)}, f32[448,128]{1,0:T(8,128)S(1)}, u32[]{:S(2)}, u32[]{:S(2)}) collective-permute-start(f32[448,128]{1,0:T(8,128)S(1)} %get-tuple-element.42), channel_id=1, source_target_pairs={{0,96},{32,0},{64,32},{96,64},{1,97},{33,1},{65,33},{97,65},{2,98}... | collective-permute-start | bytes 688136 | tf_op jit(solution)/shard_map/ppermute | solution.py:631
  41.6 1.6 %back_through_w_out.1 = (f32[32,768]{1,0:T(8,128)S(1)}, f32[16,768]{1,0:T(8,128)}) custom-call(f32[32,768]{1,0:T(8,128)S(1)} %get-tuple-element.31.pulled_ref, f32[16,768]{1,0:T(8,128)S(1)} %get-tuple-element.32.joined_ref, bf16[4,192,768]{2,1,0:T(8,128)(2,1)S(1)} %get-tuple-element.33.high_ref, bf16[4,192,768]{2,1,0:T(8,128)(2,1)S(1)} %get-tuple-element.34.low_ref), custom_call_target="tpu_custom_call" | custom-call | flops 113246208 | bytes 3000000 | tf_op jit(solution)/shard_map/back_through_w_out/pallas_call | solution.py:439
  43.2 8.1 %encoder_backward.1 = (f32[768,768]{1,0:T(8,128)S(1)}, f32[3,768]{1,0:T(4,128)S(1)}) custom-call(f32[32,768]{1,0:T(8,128)S(1)} %get-tuple-element.35.back_ref, f32[1,768]{1,0:T(1,128)S(1)} %reshape.29.gain_ref, bf16[1024,768]{1,0:T(8,128)(2,1)} %bitcast.31, bf16[1024,768]{1,0:T(8,128)(2,1)} %copy-done.6, f32[2048,768]{1,0:T(8,128)} %get-tuple-element.36.slope_ref), custom_call_target="tpu_custom_call" | custom-call | flops 6039797760 | bytes 4000000 | tf_op jit(solution)/shard_map/encoder_backward/pallas_call | solution.py:496
  51.3 0.0 collective-permute-done.4.rest_1_
  51.3 0.0 collective-permute-done.5.rest_2_
  51.4 0.0 collective-permute-done.6.rest_3_
  51.4 0.9 finish_gradients.1
  52.3 0.2 convert_element_type.9
  52.5 30.3 %all_to_all.10 = f16[16,416,128]{2,1,0:T(8,128)(2,1)S(1)} all-to-all(f16[16,416,128]{2,1,0:T(8,128)(2,1)S(1)} %bitcast.23), channel_id=1, replica_groups=mesh['z'=4,'core'=2,'x'=4,'y'=4] {'x','y'}, dimensions={0} | all-to-all | bytes 3407872 | tf_op jit(solution)/shard_map/all_to_all | solution.py:636
  82.8 0.3 convert_element_type.11.came_ref
  83.1 0.0 copy-start
  83.1 0.0 copy-start.2
  83.1 1.7 %plane_sums.1 = (f32[12,768]{1,0:T(8,128)}, f32[4,192,128]{2,1,0:T(8,128)S(1)}, f32[72,128]{1,0:T(8,128)S(1)}, f32[72,128]{1,0:T(8,128)S(1)}, f32[72,128]{1,0:T(8,128)S(1)}, /*index=5*/f32[72,128]{1,0:T(8,128)S(1)}) custom-call(s32[5]{0:T(128)S(1)} %stack.29.place_ref, f32[16,416,128]{2,1,0:T(8,128)S(1)} %convert_element_type.11.came_ref), custom_call_target="tpu_custom_call" | custom-call | flops 10000000 | bytes 4000000 | tf_op jit(solution)/shard_map/plane_sums/pallas_call | solution.py:594
  84.8 0.0 collective-permute-start.7
  84.8 0.7 collective-permute-start.8
  85.5 3.3 %collective-permute-start.9 = (f32[72,128]{1,0:T(8,128)S(1)}, f32[72,128]{1,0:T(8,128)S(1)}, u32[]{:S(2)}, u32[]{:S(2)}) collective-permute-start(f32[72,128]{1,0:T(8,128)S(1)} %get-tuple-element.47), channel_id=1, source_target_pairs={{0,64},{32,96},{64,0},{96,32},{1,65},{33,97},{65,1},{97,33},{2,66}... | collective-permute-start | bytes 110600 | tf_op jit(solution)/shard_map/ppermute | solution.py:631
  88.8 0.6 collective-permute-start.10
  89.4 0.0 collective-permute-done.7.other_ref
  89.4 0.0 copy-done
  89.4 0.0 copy-done.2
  89.4 2.5 %slot_scores.1.rest_4_ = f32[512,256]{1,0:T(8,128)} custom-call(s32[5]{0:T(128)S(1)} %stack.29.place_ref, s32[4,512]{1,0:T(4,128)S(1)} %bitcast.22, f32[512,768]{1,0:T(8,128)S(1)} %copy-done, f32[768,128]{1,0:T(8,128)S(1)} %bitcast.20, f32[768,128]{1,0:T(8,128)S(1)} %collective-permute-done.7.other_ref), custom_call_target="tpu_custom_call" | custom-call | flops 603979776 | bytes 4000000 | tf_op jit(solution)/shard_map/slot_scores/pallas_call | solution.py:355
  91.9 0.0 collective-permute-done.8.rest_1_
  91.9 0.0 collective-permute-done.9.rest_2_
  91.9 0.8 collective-permute-done.10.rest_3_
  92.7 0.6 z_sums.1
  (2 shorter events, 0.0 us)
Async XLA Ops:
  0.6 17.3 %collective-permute-start.2 = (bf16[1024,768]{1,0:T(8,128)(2,1)}, bf16[1024,768]{1,0:T(8,128)(2,1)S(1)}, u32[]{:S(2)}, u32[]{:S(2)}) collective-permute-start(bf16[1024,768]{1,0:T(8,128)(2,1)} %bitcast.29), channel_id=1, source_target_pairs={{0,16},{16,0},{1,17},{17,1},{2,18},{18,2},{3,19},{19,3},{4,20},{20... | collective-permute-start | bytes 4718600 | tf_op jit(solution)/shard_map/ppermute | solution.py:627
  1.4 16.5 %collective-permute-start = (s32[2,16]{1,0:T(2,128)S(1)}, s32[2,16]{1,0:T(2,128)S(1)}, u32[]{:S(2)}, u32[]{:S(2)}) collective-permute-start(s32[2,16]{1,0:T(2,128)S(1)} %pad_add_fusion), channel_id=1, source_target_pairs={{0,16},{16,0},{1,17},{17,1},{2,18},{18,2},{3,19},{19,3},{4,20},{20... | collective-permute-start | bytes 392 | tf_op jit(solution)/shard_map/ppermute | solution.py:627
  2.0 15.9 %copy-start.3 = (f32[768]{0:T(1024)S(1)}, f32[768]{0:T(1024)}, u32[]{:S(2)}) copy-start(f32[768]{0:T(1024)} %param.13) | copy-start | bytes 9220
  2.0 15.9 %copy-start.4 = (s32[16]{0:T(128)S(1)}, s32[16]{0:T(128)}, u32[]{:S(2)}) copy-start(s32[16]{0:T(128)} %param.11) | copy-start | bytes 196
  6.2 27.7 %all-to-all-start = ((f32[64,24,128]{2,1,0:T(8,128)}), f32[64,24,128]{2,1,0:T(8,128)S(1)}, u32[]{:S(2)}, u32[]{:S(2)}) async-start(f32[64,24,128]{2,1,0:T(8,128)} %bitcast.10), calls=%async_computation | async-start | bytes 1572864 | tf_op jit(solution)/shard_map/all_to_all | solution.py:636
  18.0 1.2 %copy-start.6 = (bf16[1024,768]{1,0:T(8,128)(2,1)}, bf16[1024,768]{1,0:T(8,128)(2,1)S(1)}, u32[]{:S(2)}) copy-start(bf16[1024,768]{1,0:T(8,128)(2,1)S(1)} %collective-permute-done.2.other_ref) | copy-start | bytes 4718596
  19.1 13.7 %copy-start.5 = (s32[16,1]{0,1:T(1,128)S(1)}, s32[16,1]{0,1:T(1,128)}, u32[]{:S(2)}) copy-start(s32[16,1]{0,1:T(1,128)} %param.12) | copy-start | bytes 196
  19.1 15.5 %copy-start.1 = (f32[16,768]{1,0:T(8,128)S(1)}, f32[16,768]{1,0:T(8,128)}, u32[]{:S(2)}) copy-start(f32[16,768]{1,0:T(8,128)} %free_ref.1) | copy-start | bytes 147460
  32.8 1.9 %collective-permute-start.3 = (f32[32,768]{1,0:T(8,128)S(1)}, f32[32,768]{1,0:T(8,128)S(1)}, u32[]{:S(2)}, u32[]{:S(2)}) collective-permute-start(f32[32,768]{1,0:T(8,128)S(1)} %get-tuple-element.27.part_ref), channel_id=1, source_target_pairs={{0,16},{16,0},{1,17},{17,1},{2,18},{18,2},{3,19},{19,3},{4,20},{20... | collective-permute-start | bytes 294920 | tf_op jit(solution)/shard_map/ppermute | solution.py:627
  34.6 1.4 %collective-permute-start.1 = (f32[32,768]{1,0:T(8,128)S(1)}, f32[32,768]{1,0:T(8,128)S(1)}, u32[]{:S(2)}, u32[]{:S(2)}) collective-permute-start(f32[32,768]{1,0:T(8,128)S(1)} %returned_gradients.1.free_ref), channel_id=1, source_target_pairs={{0,16},{16,0},{1,17},{17,1},{2,18},{18,2},{3,19},{19,3},{4,20},{20... | collective-permute-start | bytes 294920 | tf_op jit(solution)/shard_map/ppermute | solution.py:627
  36.6 14.7 %collective-permute-start.4 = (f32[448,128]{1,0:T(8,128)S(1)}, f32[448,128]{1,0:T(8,128)S(1)}, u32[]{:S(2)}, u32[]{:S(2)}) collective-permute-start(f32[448,128]{1,0:T(8,128)S(1)} %get-tuple-element.40), channel_id=1, source_target_pairs={{0,32},{32,64},{64,96},{96,0},{1,33},{33,65},{65,97},{97,1},{2,34}... | collective-permute-start | bytes 688136 | tf_op jit(solution)/shard_map/ppermute | solution.py:631
  37.4 14.0 %collective-permute-start.5 = (f32[448,128]{1,0:T(8,128)S(1)}, f32[448,128]{1,0:T(8,128)S(1)}, u32[]{:S(2)}, u32[]{:S(2)}) collective-permute-start(f32[448,128]{1,0:T(8,128)S(1)} %get-tuple-element.41), channel_id=1, source_target_pairs={{0,64},{32,96},{64,0},{96,32},{1,65},{33,97},{65,1},{97,33},{2,66}... | collective-permute-start | bytes 688136 | tf_op jit(solution)/shard_map/ppermute | solution.py:631
  40.2 11.1 %collective-permute-start.6 = (f32[448,128]{1,0:T(8,128)S(1)}, f32[448,128]{1,0:T(8,128)S(1)}, u32[]{:S(2)}, u32[]{:S(2)}) collective-permute-start(f32[448,128]{1,0:T(8,128)S(1)} %get-tuple-element.42), channel_id=1, source_target_pairs={{0,96},{32,0},{64,32},{96,64},{1,97},{33,1},{65,33},{97,65},{2,98}... | collective-permute-start | bytes 688136 | tf_op jit(solution)/shard_map/ppermute | solution.py:631
  83.1 6.3 %copy-start = (f32[512,768]{1,0:T(8,128)S(1)}, f32[512,768]{1,0:T(8,128)}, u32[]{:S(2)}) copy-start(f32[512,768]{1,0:T(8,128)} %queries_ref.3) | copy-start | bytes 4718596
  83.1 6.3 %copy-start.2 = (s32[512,4]{0,1:T(4,128)S(1)}, s32[512,4]{0,1:T(4,128)}, u32[]{:S(2)}) copy-start(s32[512,4]{0,1:T(4,128)} %param.18) | copy-start | bytes 24580
  84.8 4.6 %collective-permute-start.7 = (f32[768,128]{1,0:T(8,128)S(1)}, f32[768,128]{1,0:T(8,128)S(1)}, u32[]{:S(2)}, u32[]{:S(2)}) collective-permute-start(f32[768,128]{1,0:T(8,128)S(1)} %bitcast.19), channel_id=1, source_target_pairs={{0,16},{16,0},{1,17},{17,1},{2,18},{18,2},{3,19},{19,3},{4,20},{20... | collective-permute-start | bytes 1179656 | tf_op jit(solution)/shard_map/ppermute | solution.py:627
  84.8 7.1 %collective-permute-start.8 = (f32[72,128]{1,0:T(8,128)S(1)}, f32[72,128]{1,0:T(8,128)S(1)}, u32[]{:S(2)}, u32[]{:S(2)}) collective-permute-start(f32[72,128]{1,0:T(8,128)S(1)} %get-tuple-element.46), channel_id=1, source_target_pairs={{0,32},{32,64},{64,96},{96,0},{1,33},{33,65},{65,97},{97,1},{2,34}... | collective-permute-start | bytes 110600 | tf_op jit(solution)/shard_map/ppermute | solution.py:631
  85.5 6.4 %collective-permute-start.9 = (f32[72,128]{1,0:T(8,128)S(1)}, f32[72,128]{1,0:T(8,128)S(1)}, u32[]{:S(2)}, u32[]{:S(2)}) collective-permute-start(f32[72,128]{1,0:T(8,128)S(1)} %get-tuple-element.47), channel_id=1, source_target_pairs={{0,64},{32,96},{64,0},{96,32},{1,65},{33,97},{65,1},{97,33},{2,66}... | collective-permute-start | bytes 110600 | tf_op jit(solution)/shard_map/ppermute | solution.py:631
  88.8 4.0 %collective-permute-start.10 = (f32[72,128]{1,0:T(8,128)S(1)}, f32[72,128]{1,0:T(8,128)S(1)}, u32[]{:S(2)}, u32[]{:S(2)}) collective-permute-start(f32[72,128]{1,0:T(8,128)S(1)} %get-tuple-element.48), channel_id=1, source_target_pairs={{0,96},{32,0},{64,32},{96,64},{1,97},{33,1},{65,33},{97,65},{2,98}... | collective-permute-start | bytes 110600 | tf_op jit(solution)/shard_map/ppermute | solution.py:631
